TPU v7x, 128 devices: a whole 4x4x4 slice. The times are simulated.
128 devices in a mesh: grp: 16 (over z_hi, x, core), blk: 8 (over y, z_lo).
Axes of the slice: x: 4, y: 4, z: 4 (z_hi: 2, z_lo: 2; z = z_hi * 2 + z_lo), core: 2. Of those that a mesh axis runs over, the one named last changes fastest.
Arguments:
- queries: bfloat16 [32768, 2048], P(('grp', 'blk')), may hold values from -8 to 8
- keys: bfloat16 [32768, 2048], P(('grp', 'blk')), may hold values from -8 to 8
- values: bfloat16 [32768, 2048], P(('grp', 'blk')), may hold values from -6 to 6
- cluster_ids: int32 [32768], P(('grp', 'blk')), may hold values from 0 to 63, as said below
- positions: int32 [32768], P(('grp', 'blk')), may hold values from 0 to 32767, each once
Outputs:
- attended: bfloat16 [32768, 2048], P(('grp', 'blk'))
Inputs may be any that keep to these rules, and one draw needn't show every extreme that they name: `cluster_ids`: group g holds clusters g * 4 to g * 4 + 3. The 256 tokens of one device lie in the clusters of one group at most 32 times; for each index along blk, one group drawn from the seed receives exactly 32 tokens from every device with that index.
All inputs are finite; a program needn't handle non-finite values.
Results may differ from a plain program's by a relative error of at most 0.007.
Values may be sent and summed in bfloat16 or wider, within the bound.
No kernel may reach another device: no remote copies, remote signals or barrier semaphores. Data moves between devices by JAX's collectives and lax.ppermute only.
A program may use at most 192 MiB of HBM per device.

v0:
```python
import math

import jax
import jax.numpy as jnp
from jax import lax
from jax.sharding import PartitionSpec as P

HEAD_DIM = 128
CL_GRP = 4


def shortened(array):

    def short(part):
        return part.astype(jnp.bfloat16) if part.dtype == jnp.float32 else part

    return jax.tree.map(short, array)


def absorb(
    state, query_heads, query_cluster, query_place, key_heads, value_heads, key_cluster, key_place
):
    row_max, totals, summed = state
    scores = jnp.einsum(
        "qhd,khd->hqk", query_heads, key_heads, preferred_element_type=jnp.float32
    ) * HEAD_DIM ** (-0.5)
    visible = (key_cluster[None, :] == query_cluster[:, None]) & (
        key_place[None, :] <= query_place[:, None]
    )
    masked = jnp.where(visible[None], scores, -1e30)
    fresh = jnp.maximum(row_max, jnp.max(masked, axis=2))
    weight = jnp.where(visible[None], jnp.exp(scores - fresh[:, :, None]), 0.0)
    rescale = jnp.exp(row_max - fresh)
    totals = totals * rescale + jnp.sum(weight, axis=2)
    summed = summed * rescale[:, :, None] + jnp.einsum(
        "hqk,khd->hqd", weight.astype(jnp.bfloat16), value_heads, preferred_element_type=jnp.float32
    )
    return (fresh, totals, summed)


def sweep(
    state, query_heads, query_cluster, query_place, key_rows, value_rows, key_cluster, key_place
):
    key_total = key_rows.shape[0]
    heads = query_heads.shape[1]
    block_rows = math.gcd(key_total, 512)
    block_count = key_total // block_rows

    def absorb_block(number, carried):
        offset = number * block_rows
        key_heads = lax.dynamic_slice_in_dim(key_rows, offset, block_rows, 0).reshape(
            block_rows, heads, HEAD_DIM
        )
        value_heads = lax.dynamic_slice_in_dim(value_rows, offset, block_rows, 0).reshape(
            block_rows, heads, HEAD_DIM
        )
        return absorb(
            carried,
            query_heads,
            query_cluster,
            query_place,
            key_heads,
            value_heads,
            lax.dynamic_slice_in_dim(key_cluster, offset, block_rows, 0),
            lax.dynamic_slice_in_dim(key_place, offset, block_rows, 0),
        )

    return lax.fori_loop(0, block_count, absorb_block, state)


def route_slots(target, group_count):
    onehot = (target[:, None] == jnp.arange(group_count, dtype=jnp.int32)[None, :]).astype(
        jnp.int32
    )
    before = jnp.cumsum(onehot, axis=0) - onehot
    return jnp.sum(before * onehot, axis=1)


def place_rows(source, slot_index, slot_total, filler):
    return (
        jnp.full((slot_total,) + source.shape[1:], filler, source.dtype).at[slot_index].set(source)
    )


def local(queries, keys, values, cluster_ids, positions):
    tok_rows, width = queries.shape
    group_count = lax.axis_size("grp")
    capacity = 2 * tok_rows // group_count
    heads = width // HEAD_DIM
    slot_total = group_count * capacity
    target = cluster_ids // CL_GRP
    slot_index = target * capacity + route_slots(target, group_count)
    query_buffer = place_rows(queries, slot_index, slot_total, 0)
    cluster_buffer = place_rows(cluster_ids, slot_index, slot_total, -1)
    place_buffer = place_rows(positions, slot_index, slot_total, 0)
    initial = (
        jnp.full((heads, slot_total), -1e30, jnp.float32),
        jnp.zeros((heads, slot_total), jnp.float32),
        jnp.zeros((heads, slot_total, HEAD_DIM), jnp.float32),
    )
    key_buffer = place_rows(keys, slot_index, slot_total, 0)
    value_buffer = place_rows(values, slot_index, slot_total, 0)
    query_in, key_in, value_in, cluster_in, place_in = (
        lax.all_to_all(query_buffer, "grp", split_axis=0, concat_axis=0, tiled=True),
        lax.all_to_all(key_buffer, "grp", split_axis=0, concat_axis=0, tiled=True),
        lax.all_to_all(value_buffer, "grp", split_axis=0, concat_axis=0, tiled=True),
        lax.all_to_all(cluster_buffer, "grp", split_axis=0, concat_axis=0, tiled=True),
        lax.all_to_all(place_buffer, "grp", split_axis=0, concat_axis=0, tiled=True),
    )
    query_in, key_in, value_in, cluster_in, place_in = (
        query_in,
        key_in,
        value_in,
        cluster_in,
        place_in,
    )
    query_heads = query_in.reshape(slot_total, heads, HEAD_DIM)
    state = sweep(
        initial,
        query_heads,
        cluster_in,
        place_in,
        lax.all_gather(key_in, "blk", axis=0, tiled=True),
        lax.all_gather(value_in, "blk", axis=0, tiled=True),
        lax.all_gather(shortened(cluster_in), "blk", axis=0, tiled=True),
        lax.all_gather(shortened(place_in), "blk", axis=0, tiled=True),
    )
    row_max, totals, summed = state
    safe_totals = jnp.where(totals > 0.0, totals, 1.0)
    result = (
        (summed / safe_totals[:, :, None])
        .transpose(1, 0, 2)
        .reshape(slot_total, width)
        .astype(jnp.bfloat16)
    )
    returned = lax.all_to_all(result, "grp", split_axis=0, concat_axis=0, tiled=True)
    return returned[slot_index]


def solution(mesh):
    placed = (
        P(("grp", "blk"), None),
        P(("grp", "blk"), None),
        P(("grp", "blk"), None),
        P(("grp", "blk")),
        P(("grp", "blk")),
    )
    return jax.shard_map(
        local, mesh=mesh, in_specs=placed, out_specs=P(("grp", "blk"), None), check_vma=False
    )
```

profile of v0, /device:TPU:0, one launch (start us, length us, event | category | flops | bytes accessed | tf_op | source)
XLA Modules:
  0.0 1140.0 jit_solution(9870984505431983590)
XLA Ops:
  9.5 3.5 scatter_custom_fusion.2
  13.0 36.9 %all_to_all.66 = bf16[16,32,2048]{2,1,0:T(8,128)(2,1)} all-to-all(bf16[16,32,2048]{2,1,0:T(8,128)(2,1)S(1)} %bitcast.84), channel_id=1, replica_groups=mesh['grp'=16,'blk'=8] {'grp'}, dimensions={0} | all-to-all | bytes 4194304 | tf_op jit(solution)/shard_map/all_to_all | solution.py:105
  50.0 3.5 scatter_custom_fusion.4
  53.5 57.4 %all_to_all.67 = bf16[16,32,2048]{2,1,0:T(8,128)(2,1)} all-to-all(bf16[16,32,2048]{2,1,0:T(8,128)(2,1)S(1)} %bitcast.85), channel_id=1, replica_groups=mesh['grp'=16,'blk'=8] {'grp'}, dimensions={0} | all-to-all | bytes 4194304 | tf_op jit(solution)/shard_map/all_to_all | solution.py:106
  113.2 4.4 all-to-all-start
  119.8 5.4 all-to-all-done
  125.2 3.4 all-to-all-start.1
  128.6 4.4 scatter_custom_fusion.3
  133.0 3.2 all-to-all-done.1
  136.2 3.9 all-to-all-start.3
  142.3 65.8 %all-gather = s32[8,1,512]{2,1,0:T(1,128)S(1)} all-gather(s32[1,1,512]{2,1,0:T(1,128)S(1)} %reshape.163), channel_id=1, replica_groups=mesh['grp'=16,'blk'=8] {'blk'}, dimensions={0}, use_global_device_ids=true | all-gather | bytes 18432 | tf_op jit(solution)/shard_map/all_gather | solution.py:125
  208.2 44.0 %all-gather.1 = s32[8,1,512]{2,1,0:T(1,128)S(1)} all-gather(s32[1,1,512]{2,1,0:T(1,128)S(1)} %reshape.165), channel_id=1, replica_groups=mesh['grp'=16,'blk'=8] {'blk'}, dimensions={0}, use_global_device_ids=true | all-gather | bytes 18432 | tf_op jit(solution)/shard_map/all_gather | solution.py:126
  254.6 164.0 %all-gather.5.cloned.1.call-done = bf16[4096,2048]{1,0:T(8,128)(2,1)} async-done(((bf16[512,2048]{1,0:T(8,128)(2,1)}), bf16[4096,2048]{1,0:T(8,128)(2,1)}) %all-gather.5.cloned.1.call-update) | async-done | bytes 16777232 | tf_op jit(solution)/shard_map/all_gather | solution.py:123
  418.6 328.4 %all-gather.7.cloned.1.call-done = bf16[4096,2048]{1,0:T(8,128)(2,1)} async-done(((bf16[512,2048]{1,0:T(8,128)(2,1)}), bf16[4096,2048]{1,0:T(8,128)(2,1)}) %all-gather.7.cloned.1.call-update) | async-done | bytes 16777232 | tf_op jit(solution)/shard_map/all_gather | solution.py:124
  747.0 341.2 %while.18 = (s32[]{:T(128)}, f32[16,512]{1,0:T(8,128)S(1)}, f32[16,512]{1,0:T(8,128)S(1)}, f32[16,512,128]{2,1,0:T(8,128)}, s32[4096]{0:T(1024)S(1)}, /*index=5*...) while((s32[]{:T(128)}, f32[16,512]{1,0:T(8,128)S(1)}, ...), condition=%wide.region_11.12_spmd.clone, body=%wide.region_8.11_spmd.clone.sunk | while | flops 2197594112 | bytes 83378384 | solution.py:68
  747.4 4.0 constant_dynamic-slice_fusion.3
  751.4 3.9 copy.43
  755.3 11.0 fusion.48
  766.4 9.2 fusion.49
  775.5 2.6 copy.44
  778.1 10.8 fusion.51
  789.3 4.0 constant_dynamic-slice_fusion.3
  793.3 3.9 copy.43
  797.2 11.0 fusion.48
  808.2 9.2 fusion.49
  817.4 2.6 copy.44
  820.0 11.6 %fusion.51 = f32[16,512,128]{2,1,0:T(8,128)} fusion(f32[16,512,128]{2,1,0:T(8,128)} %get-tuple-element.386, f32[16,512]{1,0:T(8,128)S(1)} %get-tuple-element.366, pred[]{:T(512)S(6)} %compare.5, bf16[512,16,128]{0,2,1:T(8,128)(2,1)} %bitcast.79, f32[16,512,512]{2,1,0:T(8,128)} %get-tuple-element.364, f32[16,512]{1,0:T(8,128)S(1)} %select_maximum_fusion.2, ...), kind=kOutput, calls=%fused_computation.19.clone.1 | convolution fusion | flops 1093664768 | bytes 27590656 | tf_op jit(solution)/shard_map/while/body/eval_jaxpr/hqk,khd->hqd/dot_general | solution.py:35
  832.1 4.0 constant_dynamic-slice_fusion.3
  836.1 3.9 copy.43
  840.0 11.0 fusion.48
  851.0 9.2 fusion.49
  860.2 2.6 copy.44
  862.7 11.6 %fusion.51 = f32[16,512,128]{2,1,0:T(8,128)} fusion(f32[16,512,128]{2,1,0:T(8,128)} %get-tuple-element.386, f32[16,512]{1,0:T(8,128)S(1)} %get-tuple-element.366, pred[]{:T(512)S(6)} %compare.5, bf16[512,16,128]{0,2,1:T(8,128)(2,1)} %bitcast.79, f32[16,512,512]{2,1,0:T(8,128)} %get-tuple-element.364, f32[16,512]{1,0:T(8,128)S(1)} %select_maximum_fusion.2, ...), kind=kOutput, calls=%fused_computation.19.clone.1 | convolution fusion | flops 1093664768 | bytes 27590656 | tf_op jit(solution)/shard_map/while/body/eval_jaxpr/hqk,khd->hqd/dot_general | solution.py:35
  874.8 4.0 constant_dynamic-slice_fusion.3
  878.8 3.9 copy.43
  882.7 11.0 fusion.48
  893.7 9.2 fusion.49
  902.9 2.6 copy.44
  905.5 11.6 %fusion.51 = f32[16,512,128]{2,1,0:T(8,128)} fusion(f32[16,512,128]{2,1,0:T(8,128)} %get-tuple-element.386, f32[16,512]{1,0:T(8,128)S(1)} %get-tuple-element.366, pred[]{:T(512)S(6)} %compare.5, bf16[512,16,128]{0,2,1:T(8,128)(2,1)} %bitcast.79, f32[16,512,512]{2,1,0:T(8,128)} %get-tuple-element.364, f32[16,512]{1,0:T(8,128)S(1)} %select_maximum_fusion.2, ...), kind=kOutput, calls=%fused_computation.19.clone.1 | convolution fusion | flops 1093664768 | bytes 27590656 | tf_op jit(solution)/shard_map/while/body/eval_jaxpr/hqk,khd->hqd/dot_general | solution.py:35
  917.6 4.1 constant_dynamic-slice_fusion.3
  921.6 3.9 copy.43
  925.5 11.0 fusion.48
  936.6 9.2 fusion.49
  945.7 2.6 copy.44
  948.3 11.6 %fusion.51 = f32[16,512,128]{2,1,0:T(8,128)} fusion(f32[16,512,128]{2,1,0:T(8,128)} %get-tuple-element.386, f32[16,512]{1,0:T(8,128)S(1)} %get-tuple-element.366, pred[]{:T(512)S(6)} %compare.5, bf16[512,16,128]{0,2,1:T(8,128)(2,1)} %bitcast.79, f32[16,512,512]{2,1,0:T(8,128)} %get-tuple-element.364, f32[16,512]{1,0:T(8,128)S(1)} %select_maximum_fusion.2, ...), kind=kOutput, calls=%fused_computation.19.clone.1 | convolution fusion | flops 1093664768 | bytes 27590656 | tf_op jit(solution)/shard_map/while/body/eval_jaxpr/hqk,khd->hqd/dot_general | solution.py:35
  960.4 4.0 constant_dynamic-slice_fusion.3
  964.4 3.9 copy.43
  968.3 11.0 fusion.48
  979.3 9.2 fusion.49
  988.5 2.6 copy.44
  991.1 11.6 %fusion.51 = f32[16,512,128]{2,1,0:T(8,128)} fusion(f32[16,512,128]{2,1,0:T(8,128)} %get-tuple-element.386, f32[16,512]{1,0:T(8,128)S(1)} %get-tuple-element.366, pred[]{:T(512)S(6)} %compare.5, bf16[512,16,128]{0,2,1:T(8,128)(2,1)} %bitcast.79, f32[16,512,512]{2,1,0:T(8,128)} %get-tuple-element.364, f32[16,512]{1,0:T(8,128)S(1)} %select_maximum_fusion.2, ...), kind=kOutput, calls=%fused_computation.19.clone.1 | convolution fusion | flops 1093664768 | bytes 27590656 | tf_op jit(solution)/shard_map/while/body/eval_jaxpr/hqk,khd->hqd/dot_general | solution.py:35
  1003.1 4.0 constant_dynamic-slice_fusion.3
  1007.1 3.9 copy.43
  1011.1 11.0 fusion.48
  1022.1 9.2 fusion.49
  1033.8 11.6 %fusion.51 = f32[16,512,128]{2,1,0:T(8,128)} fusion(f32[16,512,128]{2,1,0:T(8,128)} %get-tuple-element.386, f32[16,512]{1,0:T(8,128)S(1)} %get-tuple-element.366, pred[]{:T(512)S(6)} %compare.5, bf16[512,16,128]{0,2,1:T(8,128)(2,1)} %bitcast.79, f32[16,512,512]{2,1,0:T(8,128)} %get-tuple-element.364, f32[16,512]{1,0:T(8,128)S(1)} %select_maximum_fusion.2, ...), kind=kOutput, calls=%fused_computation.19.clone.1 | convolution fusion | flops 1093664768 | bytes 27590656 | tf_op jit(solution)/shard_map/while/body/eval_jaxpr/hqk,khd->hqd/dot_general | solution.py:35
  1045.9 4.0 constant_dynamic-slice_fusion.3
  1049.9 3.9 copy.43
  1053.8 11.0 fusion.48
  1064.8 9.2 fusion.49
  1076.6 11.6 %fusion.51 = f32[16,512,128]{2,1,0:T(8,128)} fusion(f32[16,512,128]{2,1,0:T(8,128)} %get-tuple-element.386, f32[16,512]{1,0:T(8,128)S(1)} %get-tuple-element.366, pred[]{:T(512)S(6)} %compare.5, bf16[512,16,128]{0,2,1:T(8,128)(2,1)} %bitcast.79, f32[16,512,512]{2,1,0:T(8,128)} %get-tuple-element.364, f32[16,512]{1,0:T(8,128)S(1)} %select_maximum_fusion.2, ...), kind=kOutput, calls=%fused_computation.19.clone.1 | convolution fusion | flops 1093664768 | bytes 27590656 | tf_op jit(solution)/shard_map/while/body/eval_jaxpr/hqk,khd->hqd/dot_general | solution.py:35
  1088.2 3.1 fusion.17
  1095.0 6.6 all-to-all-start.5
  1101.7 29.2 %all-to-all-done.5 = bf16[16,32,2048]{2,1,0:T(8,128)(2,1)S(1)} async-done(((bf16[16,32,2048]{2,1,0:T(8,128)(2,1)}), bf16[16,32,2048]{2,1,0:T(8,128)(2,1)S(1)}, u32[]{:S(2)}, u32[]{:S(2)}) %all-to-all-start.5) | async-done | bytes 2097184 | tf_op jit(solution)/shard_map/all_to_all | solution.py:136
  (85 shorter events, 26.9 us)
Async XLA Ops:
  6.5 412.1 %all-gather.5.cloned.1.call-start = ((), (), s32[]{:S(2)}) async-start(), calls=%async_computation.6 | async-start | bytes 18874368 | tf_op jit(solution)/shard_map/all_gather | solution.py:123
  50.0 697.0 %all-gather.7.cloned.1.call-start = ((), (), s32[]{:S(2)}) async-start(), calls=%async_computation.7 | async-start | bytes 18874368 | tf_op jit(solution)/shard_map/all_gather | solution.py:124
  113.2 12.0 %all-to-all-start = ((s32[16,32,1]{1,2,0:T(1,128)}), s32[16,32,1]{1,2,0:T(1,128)S(1)}, u32[]{:S(2)}, u32[]{:S(2)}) async-start(s32[16,32,1]{1,2,0:T(1,128)} %bitcast.2), calls=%async_computation | async-start | bytes 16384 | tf_op jit(solution)/shard_map/all_to_all | solution.py:107
  125.2 11.0 all-to-all-start.1
  136.2 115.9 %all-to-all-start.3 = ((bf16[16,32,2048]{2,1,0:T(8,128)(2,1)}), bf16[16,32,2048]{2,1,0:T(8,128)(2,1)S(1)}, u32[]{:S(2)}, u32[]{:S(2)}) async-start(bf16[16,32,2048]{2,1,0:T(8,128)(2,1)} %bitcast.8), calls=%async_computation.3 | async-start | bytes 4194304 | tf_op jit(solution)/shard_map/all_to_all | solution.py:104
  1095.0 35.9 %all-to-all-start.5 = ((bf16[16,32,2048]{2,1,0:T(8,128)(2,1)}), bf16[16,32,2048]{2,1,0:T(8,128)(2,1)S(1)}, u32[]{:S(2)}, u32[]{:S(2)}) async-start(bf16[16,32,2048]{2,1,0:T(8,128)(2,1)} %convert_element_type.28), calls=%async_computation.5 | async-start | bytes 4194304 | tf_op jit(solution)/shard_map/all_to_all | solution.py:136
Sparse Core Ops, SparseCore 0:
  50.1 368.4 all-gather.4
  420.3 326.6 all-gather.6
where the time goes:
time: 1140 us
  waiting for transfers between devices  530 us (46%)
  blocking collectives  204 us (18%)
  matrix products  180 us (16%)
  local copies, waits for them, and re-layouts  111 us (10%)
  other arithmetic  82.8 us (7%)
  starting transfers between devices  18.4 us (2%)
  between operations  13.5 us (1%)
    all_gather x1, waiting for transfers between devices, local(): lax.all_gather(value_in, 'blk', axis=0, tiled=True)  328 us
    all_gather x1, waiting for transfers between devices, local(): lax.all_gather(key_in, 'blk', axis=0, tiled=True)  164 us
    dot_general x8, matrix products, absorb(): jnp.einsum('hqk,khd->hqd', weight.astype(jnp.bfloat16), value_heads, pref...  92.2 us
    dot_general x8, matrix products, absorb(): jnp.einsum('qhd,khd->hqk', query_heads, key_heads, preferred_element_type...  88 us
    reduce_sum x8, other arithmetic, absorb(): totals = totals * rescale + jnp.sum(weight, axis=2)  73.2 us
    all_gather x1, blocking collectives, local(): lax.all_gather(shortened(cluster_in), 'blk', axis=0, tiled=True)  65.8 us
    all_to_all x1, blocking collectives, local(): lax.all_to_all(value_buffer, 'grp', split_axis=0, concat_axis=0, tiled=True)  57.4 us
    dynamic_slice x16, local copies, waits for them, and re-layouts, absorb_block(): lax.dynamic_slice_in_dim(value_rows, offset, block_rows, 0)  52.6 us
  transfers between devices with their start and end apart: 6, of which 5 were waited for; matrix products, arithmetic and copies ran while one was open for 1% of the time, Pallas kernels for 0%

commit v1 on v0

v1 whole, which is shorter than its diff:
```python
import functools

import jax
import jax.numpy as jnp
from jax import lax
from jax.experimental import pallas as pl
from jax.experimental.pallas import tpu as pltpu
from jax.sharding import PartitionSpec as P

HEAD_DIM = 128
CL_GRP = 4
CL_SET = 2 * CL_GRP
RUN = 48
CODES = CL_SET * RUN
BLK = 256
F32 = jnp.float32
BF16 = jnp.bfloat16
HIDDEN = -1e30


def chunk_rows(slots):
    return -(-(3 * slots + 8) // 16) * 16


def iota(shape, dim):
    return lax.broadcasted_iota(jnp.int32, shape, dim).astype(F32)


def column(row):
    return jnp.transpose(jnp.broadcast_to(row, (128, row.shape[1])))


def nt_dot(a, b):
    return lax.dot_general(a, b, (((1,), (1,)), ((), ())), preferred_element_type=F32)


def dot(a, b):
    return jnp.dot(a, b, preferred_element_type=F32)


def pack_kernel(slots, sets, parity_ref, cid_ref, pos_ref, q_ref, k_ref, v_ref, out_ref, slot_ref, place, meta):
    tokens = cid_ref.shape[1]

    @pl.when(pl.program_id(0) == 0)
    def _():
        cid = cid_ref[...]
        pos = pos_ref[...]
        own = jnp.bitwise_and(cid, CL_SET - 1)
        group = (cid - own).astype(F32) * (1.0 / CL_SET)
        key = cid.astype(F32) * tokens + iota((1, tokens), 1)
        keys = column(key)
        keys = jnp.concatenate([keys] * (tokens // 128), axis=1)
        below = keys < key
        rank = jnp.sum(jnp.where(below & (keys >= group * (CL_SET * tokens)), 1.0, 0.0), axis=0, keepdims=True)
        within = jnp.sum(jnp.where(below & (keys >= cid.astype(F32) * tokens), 1.0, 0.0), axis=0, keepdims=True)
        fits = rank < slots
        slot = jnp.where(fits, group * slots + rank, -1.0)
        slot_ref[...] = slot
        place[...] = jnp.where(iota((sets * slots, tokens), 0) == slot, 1.0, 0.0).astype(BF16)
        lane = jnp.where(fits, group * 128 + rank + 64 * parity_ref[0, 0].astype(F32), -1.0)
        spread = jnp.where(iota((sets * 128, tokens), 0) == lane, 1.0, 0.0).astype(BF16)
        low = jnp.bitwise_and(pos, 255)
        high = jnp.right_shift(pos, 8) + 1
        row = lax.broadcasted_iota(jnp.int32, (16, tokens), 0)
        facts = jnp.where(
            row == 0,
            high.astype(F32),
            jnp.where(row == 1, low.astype(F32), jnp.where(row == 2, own.astype(F32) + 1.0, jnp.where(row == 3, within, 0.0))),
        ).astype(BF16)
        meta[...] = nt_dot(facts, spread)

    x = jnp.concatenate([q_ref[...], k_ref[...], v_ref[...]], axis=1)
    y = dot(place[...], x)
    gap = out_ref.shape[2] - 3 * slots - 8
    for s in range(sets):
        part = y[s * slots : (s + 1) * slots]
        pieces = [part[:, :128], part[:, 128:256], part[:, 256:]]
        if gap:
            pieces.append(jnp.zeros((gap, 128), F32))
        pieces.append(meta[0:8, s * 128 : (s + 1) * 128])
        out_ref[s, 0] = jnp.concatenate(pieces, axis=0).astype(BF16)


def attend_kernel(slots, x_ref, o_ref, xs, ps, os, kp, code, high, low, tab_v, tab, sem):
    sources, rows, _ = x_ref.shape
    blocks = sources // 4
    total_rows = xs.shape[0]

    facts = x_ref[:, rows - 16 : rows, :].astype(F32)
    high[...] = facts[:, 8, :]
    low[...] = facts[:, 9, :]
    own = facts[:, 10, :]
    within = facts[:, 11, :]
    lane = iota((sources, 128), 1)
    counts = jnp.zeros((sources, 128), F32)
    for c in range(CL_SET):
        n = jnp.sum(jnp.where(own == c + 1, 1.0, 0.0), axis=1, keepdims=True)
        counts = counts + jnp.where(lane == c, n, 0.0)
    counts16 = counts.astype(BF16)
    r = lax.broadcasted_iota(jnp.int32, (sources, sources), 0)
    s = lax.broadcasted_iota(jnp.int32, (sources, sources), 1)

    def picked(mask):
        return dot(jnp.where(mask, 1.0, 0.0).astype(BF16), counts16)

    first = jnp.bitwise_and(r, -4)
    before = picked(s < r)
    before_block = picked(s < first)
    after_block = picked(s < first + 4)
    total = picked(s >= 0)
    nblk = jnp.floor((total + (BLK - 1)) * (1.0 / BLK))
    start_blk = dot(nblk.astype(BF16), jnp.where((r < s) & (r < CL_SET), 1.0, 0.0).astype(BF16))
    base = start_blk * BLK
    aligned = base + jnp.floor(before_block * (1.0 / 16)) * 16
    shift = base + before - aligned
    passes = jnp.where(lane < CL_SET, jnp.floor((base + after_block - aligned + (RUN - 1)) * (1.0 / RUN)), 0.0)
    passes = jnp.max(passes, axis=1, keepdims=True)
    place = within
    for c in range(CL_SET):
        place = place + jnp.where(own == c + 1, shift[:, c : c + 1], 0.0)
    step = jnp.floor(place * (1.0 / RUN) + (0.5 / RUN))
    code[...] = jnp.where(own > 0.0, step * CODES + (own - 1.0) * RUN + (place - step * RUN) + 1.0, 0.0)
    last = start_blk + nblk
    used = jnp.max(jnp.where(lane < CL_SET, last, 0.0), axis=1, keepdims=True)
    table = jnp.where(lane < CL_SET, aligned, 0.0)
    table = jnp.where(lane == 8, passes, table)
    table = jnp.where(lane == 9, used, table)
    spin = jnp.zeros((sources, 128), F32)
    for c in range(CL_SET):
        spin = spin + jnp.where(lane == 16 + c, start_blk[:, c : c + 1], 0.0) + jnp.where(lane == 24 + c, nblk[:, c : c + 1], 0.0)
    tab_v[...] = (table + spin).astype(jnp.int32)
    copy = pltpu.make_async_copy(tab_v, tab, sem)
    copy.start()
    os[...] = jnp.zeros(os.shape, BF16)
    copy.wait()
    used_blocks = tab[0, 9]

    def clear(i, _):
        at = pl.ds(pl.multiple_of(i * BLK, BLK), BLK)
        xs[at, :] = jnp.zeros((BLK, xs.shape[1]), BF16)
        ps[at, :] = jnp.zeros((BLK, 128), F32)
        return 0

    lax.fori_loop(0, jnp.minimum(used_blocks + 2, total_rows // BLK), clear, 0)

    def joined(ref, b):
        return jnp.concatenate(
            [
                ref[pl.ds(4 * b, 1), :] + ref[pl.ds(4 * b + 1, 1), :],
                ref[pl.ds(4 * b + 2, 1), :] + ref[pl.ds(4 * b + 3, 1), :],
            ],
            axis=1,
        )

    which = lax.broadcasted_iota(jnp.int32, (128, 256), 0)
    code_rows = iota((CODES, 256), 0)

    def compact(b, _):
        x4 = x_ref[pl.ds(4 * b, 4)].astype(F32)
        xcat = jnp.concatenate([x4[:, i * slots : i * slots + 64].reshape(256, 128) for i in range(3)], axis=1).astype(BF16)
        row = joined(code, b)
        where_at = jnp.where(which == 0, joined(high, b), jnp.where(which == 1, joined(low, b), 0.0)).astype(BF16)

        def one(p, _):
            select = jnp.where(code_rows == row - (p * CODES + 1).astype(F32), 1.0, 0.0).astype(BF16)
            y = dot(select, xcat).astype(BF16)
            z = nt_dot(select, where_at)
            for c in range(CL_SET):
                at = pl.ds(pl.multiple_of(tab[4 * b, c] + p * RUN, 16), RUN)
                xs[at, :] = xs[at, :] + y[c * RUN : (c + 1) * RUN]
                ps[at, :] = ps[at, :] + z[c * RUN : (c + 1) * RUN]
            return 0

        lax.fori_loop(0, tab[4 * b, 8], one, 0)
        return 0

    lax.fori_loop(0, blocks, compact, 0)

    def key_places(i, _):
        t = jnp.transpose(ps[pl.ds(pl.multiple_of(i * BLK, BLK), BLK), :])
        k = t[0:1] * 256.0 + t[1:2]
        kp[pl.ds(i, 1), :] = jnp.where(k > 0.0, k, 1e9)
        return 0

    lax.fori_loop(0, used_blocks, key_places, 0)

    def cluster(c, _):
        begin = tab[0, 16 + c]
        count = tab[0, 24 + c]

        def queries(i, _):
            at = pl.ds(pl.multiple_of((begin + i) * BLK, BLK), BLK)
            q = xs[at, 0:128]
            w = ps[at, 0:2]
            qp = w[:, 0:1] * 256.0 + w[:, 1:2]

            def keys(j, carried):
                top, total, summed = carried
                kat = pl.ds(pl.multiple_of((begin + j) * BLK, BLK), BLK)
                scores = nt_dot(q, xs[kat, 128:256]) * HEAD_DIM ** (-0.5)
                scores = jnp.where(kp[pl.ds(begin + j, 1), :] <= qp, scores, HIDDEN)
                fresh = jnp.maximum(top, jnp.max(scores, axis=1, keepdims=True))
                weight = jnp.exp(scores - fresh)
                rescale = jnp.exp(top - fresh)
                total = total * rescale + jnp.sum(weight, axis=1, keepdims=True)
                summed = summed * rescale + dot(weight.astype(BF16), xs[kat, 256:384])
                return fresh, total, summed

            init = (jnp.full((BLK, 1), HIDDEN, F32), jnp.zeros((BLK, 1), F32), jnp.zeros((BLK, 128), F32))
            _, total, summed = lax.fori_loop(0, count, keys, init)
            os[at, :] = (summed / total).astype(BF16)
            return 0

        lax.fori_loop(0, count, queries, 0)
        return 0

    lax.fori_loop(0, CL_SET, cluster, 0)

    code_lanes = iota((256, CODES), 1)

    def spread(b, _):
        col = column(joined(code, b))
        col = jnp.concatenate([col] * (CODES // 128), axis=1)

        def one(p, acc):
            cat = jnp.concatenate(
                [os[pl.ds(pl.multiple_of(tab[4 * b, c] + p * RUN, 16), RUN), :] for c in range(CL_SET)], axis=0
            )
            select = jnp.where(code_lanes == col - (p * CODES + 1).astype(F32), 1.0, 0.0).astype(BF16)
            return acc + dot(select, cat)

        acc = lax.fori_loop(0, tab[4 * b, 8], one, jnp.zeros((256, 128), F32))
        o_ref[pl.ds(4 * b, 4)] = acc.reshape(4, 64, 128)[:, :slots].astype(BF16)
        return 0

    lax.fori_loop(0, blocks, spread, 0)


def unpack_kernel(slots, slot_ref, r_ref, out_ref, select):
    sets, heads = r_ref.shape[0], r_ref.shape[1]

    @pl.when(pl.program_id(0) == 0)
    def _():
        col = column(slot_ref[...])
        col = jnp.concatenate([col] * (-(-sets * slots // 128)), axis=1)[:, : sets * slots]
        select[...] = jnp.where(iota(select.shape, 1) == col, 1.0, 0.0).astype(BF16)

    for h in range(heads):
        x = r_ref[:, h].astype(F32).reshape(sets * slots, 128).astype(BF16)
        out_ref[:, h * 128 : (h + 1) * 128] = dot(select[...], x).astype(BF16)


def attention(slots, queries, keys, values, cid_row, pos_row, parity):
    tokens, width = queries.shape
    heads = width // HEAD_DIM
    sources = lax.axis_size("grp") * lax.axis_size("blk")
    sets = sources // heads
    rows = chunk_rows(slots)
    vmem = pltpu.CompilerParams(vmem_limit_bytes=56 * 2**20)
    whole = pl.BlockSpec(memory_space=pltpu.VMEM)
    one = pl.BlockSpec((tokens, HEAD_DIM), lambda h: (0, h))
    line = pl.BlockSpec((1, tokens), lambda h: (0, 0))
    sent, slot = pl.pallas_call(
        functools.partial(pack_kernel, slots, sets),
        grid=(heads,),
        in_specs=[pl.BlockSpec(memory_space=pltpu.SMEM), line, line, one, one, one],
        out_specs=[pl.BlockSpec((sets, 1, rows, 128), lambda h: (0, h, 0, 0)), line],
        out_shape=[
            jax.ShapeDtypeStruct((sets, heads, rows, 128), BF16),
            jax.ShapeDtypeStruct((1, tokens), F32),
        ],
        scratch_shapes=[pltpu.VMEM((sets * slots, tokens), BF16), pltpu.VMEM((16, sets * 128), F32)],
        compiler_params=vmem,
        name="pack",
    )(parity, cid_row, pos_row, queries, keys, values)
    got = lax.all_to_all(sent.reshape(sources, rows, 128), ("grp", "blk"), split_axis=0, concat_axis=0, tiled=True)
    total_rows = sources * slots + (CL_SET + 2) * BLK
    done = pl.pallas_call(
        functools.partial(attend_kernel, slots),
        in_specs=[whole],
        out_specs=whole,
        out_shape=jax.ShapeDtypeStruct((sources, slots, 128), BF16),
        scratch_shapes=[
            pltpu.VMEM((total_rows, 3 * HEAD_DIM), BF16),
            pltpu.VMEM((total_rows, 128), F32),
            pltpu.VMEM((total_rows, HEAD_DIM), BF16),
            pltpu.VMEM((total_rows // BLK, BLK), F32),
            pltpu.VMEM((sources, 128), F32),
            pltpu.VMEM((sources, 128), F32),
            pltpu.VMEM((sources, 128), F32),
            pltpu.VMEM((sources, 128), jnp.int32),
            pltpu.SMEM((sources, 128), jnp.int32),
            pltpu.SemaphoreType.DMA,
        ],
        compiler_params=vmem,
        name="attend",
    )(got)
    back = lax.all_to_all(done, ("grp", "blk"), split_axis=0, concat_axis=0, tiled=True)
    per = 2
    return pl.pallas_call(
        functools.partial(unpack_kernel, slots),
        grid=(heads // per,),
        in_specs=[line, pl.BlockSpec((sets, per, slots, 128), lambda h: (0, h, 0, 0))],
        out_specs=pl.BlockSpec((tokens, per * HEAD_DIM), lambda h: (0, h)),
        out_shape=jax.ShapeDtypeStruct((tokens, width), BF16),
        scratch_shapes=[pltpu.VMEM((tokens, sets * slots), BF16)],
        compiler_params=vmem,
        name="unpack",
    )(slot, back.reshape(sets, heads, slots, 128))


def local(queries, keys, values, cluster_ids, positions):
    cid_row = cluster_ids.reshape(1, -1)
    pos_row = positions.reshape(1, -1)
    me = lax.axis_index("grp") * lax.axis_size("blk") + lax.axis_index("blk")
    parity = (me % 2).astype(jnp.int32).reshape(1, 1)
    return attention(2 * 32, queries, keys, values, cid_row, pos_row, parity)


def solution(mesh):
    placed = (
        P(("grp", "blk"), None),
        P(("grp", "blk"), None),
        P(("grp", "blk"), None),
        P(("grp", "blk")),
        P(("grp", "blk")),
    )
    return jax.shard_map(
        local, mesh=mesh, in_specs=placed, out_specs=P(("grp", "blk"), None), check_vma=False
    )
```

time: 1140 us -> 218 us (0.19)
  waiting for transfers between devices: 530 us -> 0 us
  matrix products: 180 us -> 0 us
  local copies, waits for them, and re-layouts: 111 us -> 0 us
  other arithmetic: 82.8 us -> 0 us
  Pallas kernels: 0 us -> 77.2 us
  blocking collectives: 204 us -> 141 us
  starting transfers between devices: 18.4 us -> 0 us
  between operations: 13.5 us -> 0.01 us
    all_gather x2 -> x0, waiting for transfers between devices: 492 us -> none  [the longest x1 328 us: local(): lax.all_gather(value_in, 'blk', axis=0, tiled=True)]
    dot_general x16 -> x0, matrix products: 180 us -> none  [the longest x8 92.2 us: absorb(): jnp.einsum('hqk,khd->hqd', weight.astype(jnp.bfloat16), value_heads, pref...]
    all_gather x2 -> x0, blocking collectives: 110 us -> none  [the longest x1 65.8 us: local(): lax.all_gather(shortened(cluster_in), 'blk', axis=0, tiled=True)]
    dynamic_slice x40 -> x0, local copies, waits for them, and re-layouts: 85.2 us -> none  [the longest x16 52.6 us: absorb_block(): lax.dynamic_slice_in_dim(value_rows, offset, block_rows, 0)]
    pallas_call x0 -> x3, Pallas kernels: none -> 77.2 us  [the longest x1 57.8 us: attention(): pl.pallas_call(functools.partial(attend_kernel, slots), in_specs=[whole],...]
    reduce_sum x9 -> x0, other arithmetic: 73.3 us -> none  [the longest x8 73.2 us: absorb(): totals = totals * rescale + jnp.sum(weight, axis=2)]
    all_to_all x2, blocking collectives: 94.3 us -> 141 us  [the longest x1 91.4 us: attention(): lax.all_to_all(sent.reshape(sources, rows, 128), ('grp', 'blk'), split_ax...]
    all_to_all x4 -> x0, waiting for transfers between devices: 37.8 us -> none  [the longest x1 29.2 us: local(): lax.all_to_all(result, 'grp', split_axis=0, concat_axis=0, tiled=True)]
  transfers between devices with their start and end apart: 6 -> 0, of which waited for: 5 -> 0; matrix products, arithmetic and copies ran while one was open for 1% -> 0% of each run, Pallas kernels for 0% -> 0%
where the time goes in v1:
time: 218 us
  blocking collectives  141 us (65%)
  Pallas kernels  77.2 us (35%)
    all_to_all x1, blocking collectives, attention(): lax.all_to_all(sent.reshape(sources, rows, 128), ('grp', 'blk'), split_ax...  91.4 us
    pallas_call x1, Pallas kernels, attention(): pl.pallas_call(functools.partial(attend_kernel, slots), in_specs=[whole],...  57.8 us
    all_to_all x1, blocking collectives, attention(): lax.all_to_all(done, ('grp', 'blk'), split_axis=0, concat_axis=0, tiled=T...  49.3 us
    pallas_call x1, Pallas kernels, attention(): pl.pallas_call(functools.partial(pack_kernel, slots, sets), grid=(heads,)...  12.8 us
    pallas_call x1, Pallas kernels, attention(): pl.pallas_call(functools.partial(unpack_kernel, slots), grid=(heads // pe...  6.56 us

profile of v1, /device:TPU:0, one launch (start us, length us, event | category | flops | bytes accessed | tf_op | source)
XLA Modules:
  0.0 217.8 jit_solution(8529709352956202868)
XLA Ops:
  0.0 12.8 %pack.1 = (bf16[8,16,208,128]{3,2,1,0:T(8,128)(2,1)}, f32[1,256]{1,0:T(1,128)}) custom-call(s32[1,1]{1,0:T(1,128)} %bitcast.parity_ref, s32[1,256]{1,0:T(1,128)} %bitcast.7, s32[1,256]{1,0:T(1,128)} %bitcast.8, bf16[256,2048]{1,0:T(8,128)(2,1)} %q_ref.1, bf16[256,2048]{1,0:T(8,128)(2,1)} %k_ref.1, bf16[256,2048]{1,0:T(8,128)(2,1)} %v_ref.1), custom_call_target="tpu_custom_call" | custom-call | tf_op jit(solution)/shard_map/pack/pallas_call | solution.py:263
  12.8 91.4 %all_to_all.10.x_ref = bf16[128,208,128]{2,1,0:T(8,128)(2,1)} all-to-all(bf16[128,208,128]{2,1,0:T(8,128)(2,1)} %bitcast.6), channel_id=1, replica_groups=mesh['grp'=16,'blk'=8] {'grp','blk'}, dimensions={0} | all-to-all | bytes 13631488 | tf_op jit(solution)/shard_map/all_to_all | solution.py:276
  104.2 57.8 %attend.1 = bf16[128,64,128]{2,1,0:T(8,128)(2,1)} custom-call(bf16[128,208,128]{2,1,0:T(8,128)(2,1)} %all_to_all.10.x_ref), custom_call_target="tpu_custom_call" | custom-call | tf_op jit(solution)/shard_map/attend/pallas_call | solution.py:278
  162.0 49.3 %all_to_all.11 = bf16[128,64,128]{2,1,0:T(8,128)(2,1)} all-to-all(bf16[128,64,128]{2,1,0:T(8,128)(2,1)} %attend.1), channel_id=1, replica_groups=mesh['grp'=16,'blk'=8] {'grp','blk'}, dimensions={0} | all-to-all | bytes 4194304 | tf_op jit(solution)/shard_map/all_to_all | solution.py:298
  211.3 6.6 %unpack.1 = bf16[256,2048]{1,0:T(8,128)(2,1)} custom-call(f32[1,256]{1,0:T(1,128)} %get-tuple-element.7.slot_ref, bf16[8,16,64,128]{3,2,1,0:T(8,128)(2,1)} %bitcast.5), custom_call_target="tpu_custom_call" | custom-call | tf_op jit(solution)/shard_map/unpack/pallas_call | solution.py:300

commit v2 on v1

v2 whole, which is shorter than its diff:
```python
import functools

import jax
import jax.numpy as jnp
from jax import lax
from jax.experimental import pallas as pl
from jax.experimental.pallas import tpu as pltpu
from jax.sharding import PartitionSpec as P

HEAD_DIM = 128
CL_GRP = 4
CL_SET = 2 * CL_GRP
RUN = 48
CODES = CL_SET * RUN
BLK = 128
FIXED = (4, 5, 6)
UNROLL = 8
PACK = 8
UNPACK = 8
F32 = jnp.float32
BF16 = jnp.bfloat16
HIDDEN = -1e30


def chunk_rows(slots):
    return -(-(3 * slots + 8) // 16) * 16


def iota(shape, dim):
    return lax.broadcasted_iota(jnp.int32, shape, dim).astype(F32)


def column(row):
    return jnp.transpose(jnp.broadcast_to(row, (128, row.shape[1])))


def nt_dot(a, b):
    return lax.dot_general(a, b, (((1,), (1,)), ((), ())), preferred_element_type=F32)


def dot(a, b):
    return jnp.dot(a, b, preferred_element_type=F32)


def pack_kernel(slots, sets, parity_ref, cid_ref, pos_ref, q_ref, k_ref, v_ref, out_ref, slot_ref, place, meta):
    tokens = cid_ref.shape[1]

    @pl.when(pl.program_id(0) == 0)
    def _():
        cid = cid_ref[...]
        pos = pos_ref[...]
        own = jnp.bitwise_and(cid, CL_SET - 1)
        group = (cid - own).astype(F32) * (1.0 / CL_SET)
        key = cid.astype(F32) * tokens + iota((1, tokens), 1)
        keys = column(key)
        keys = jnp.concatenate([keys] * (tokens // 128), axis=1)
        below = keys < key
        rank = jnp.sum(jnp.where(below & (keys >= group * (CL_SET * tokens)), 1.0, 0.0), axis=0, keepdims=True)
        within = jnp.sum(jnp.where(below & (keys >= cid.astype(F32) * tokens), 1.0, 0.0), axis=0, keepdims=True)
        fits = rank < slots
        slot = jnp.where(fits, group * slots + rank, -1.0)
        slot_ref[...] = slot
        place[...] = jnp.where(iota((sets * slots, tokens), 0) == slot, 1.0, 0.0).astype(BF16)
        lane = jnp.where(fits, group * 128 + rank + 64 * parity_ref[0, 0].astype(F32), -1.0)
        spread = jnp.where(iota((sets * 128, tokens), 0) == lane, 1.0, 0.0).astype(BF16)
        low = jnp.bitwise_and(pos, 255)
        high = jnp.right_shift(pos, 8) + 1
        row = lax.broadcasted_iota(jnp.int32, (16, tokens), 0)
        facts = jnp.where(
            row == 0,
            high.astype(F32),
            jnp.where(row == 1, low.astype(F32), jnp.where(row == 2, own.astype(F32) + 1.0, jnp.where(row == 3, within, 0.0))),
        ).astype(BF16)
        meta[...] = nt_dot(facts, spread)

    gap = out_ref.shape[2] - 3 * slots - 8
    for h in range(out_ref.shape[1]):
        at = slice(h * HEAD_DIM, (h + 1) * HEAD_DIM)
        y = dot(place[...], jnp.concatenate([q_ref[:, at], k_ref[:, at], v_ref[:, at]], axis=1))
        for s in range(sets):
            part = y[s * slots : (s + 1) * slots]
            pieces = [part[:, :128], part[:, 128:256], part[:, 256:]]
            if gap:
                pieces.append(jnp.zeros((gap, 128), F32))
            pieces.append(meta[0:8, s * 128 : (s + 1) * 128])
            out_ref[s, h] = jnp.concatenate(pieces, axis=0).astype(BF16)


def attend_kernel(slots, x_ref, o_ref, xs, os, code, high, low, tab_v, tab, sem):
    sources, rows, _ = x_ref.shape
    blocks = sources // 4
    total_rows = xs.shape[0]

    facts = x_ref[:, rows - 16 : rows, :].astype(F32)
    high[...] = facts[:, 8, :]
    low[...] = facts[:, 9, :]
    own = facts[:, 10, :]
    within = facts[:, 11, :]
    lane = iota((sources, 128), 1)
    counts = jnp.zeros((sources, 128), F32)
    for c in range(CL_SET):
        n = jnp.sum(jnp.where(own == c + 1, 1.0, 0.0), axis=1, keepdims=True)
        counts = counts + jnp.where(lane == c, n, 0.0)
    counts16 = counts.astype(BF16)
    r = lax.broadcasted_iota(jnp.int32, (sources, sources), 0)
    s = lax.broadcasted_iota(jnp.int32, (sources, sources), 1)

    def picked(mask):
        return dot(jnp.where(mask, 1.0, 0.0).astype(BF16), counts16)

    first = jnp.bitwise_and(r, -4)
    before = picked(s < r)
    before_block = picked(s < first)
    after_block = picked(s < first + 4)
    total = picked(s >= 0)
    nblk = jnp.floor((total + (BLK - 1)) * (1.0 / BLK))
    start_blk = dot(nblk.astype(BF16), jnp.where((r < s) & (r < CL_SET), 1.0, 0.0).astype(BF16))
    base = start_blk * BLK
    aligned = base + jnp.floor(before_block * (1.0 / 16)) * 16
    shift = base + before - aligned
    passes = jnp.where(lane < CL_SET, jnp.floor((base + after_block - aligned + (RUN - 1)) * (1.0 / RUN)), 0.0)
    passes = jnp.max(passes, axis=1, keepdims=True)
    place = within
    for c in range(CL_SET):
        place = place + jnp.where(own == c + 1, shift[:, c : c + 1], 0.0)
    step = jnp.floor(place * (1.0 / RUN) + (0.5 / RUN))
    code[...] = jnp.where(own > 0.0, step * CODES + (own - 1.0) * RUN + (place - step * RUN) + 1.0, 0.0)
    last = start_blk + nblk
    used = jnp.max(jnp.where(lane < CL_SET, last, 0.0), axis=1, keepdims=True)
    table = jnp.where(lane < CL_SET, aligned, 0.0)
    table = jnp.where(lane == 8, passes, table)
    table = jnp.where(lane == 9, used, table)
    table = jnp.where(lane == 10, jnp.max(passes), table)
    spin = jnp.zeros((sources, 128), F32)
    for c in range(CL_SET):
        spin = spin + jnp.where(lane == 16 + c, start_blk[:, c : c + 1], 0.0) + jnp.where(lane == 24 + c, nblk[:, c : c + 1], 0.0)
    tab_v[...] = (table + spin).astype(jnp.int32)
    copy = pltpu.make_async_copy(tab_v, tab, sem)
    copy.start()
    os[...] = jnp.zeros(os.shape, BF16)
    copy.wait()
    used_blocks = tab[0, 9]

    def clear(i, _):
        at = pl.ds(pl.multiple_of(i * BLK, BLK), BLK)
        xs[at, :] = jnp.zeros((BLK, xs.shape[1]), BF16)
        return 0

    lax.fori_loop(0, jnp.minimum(used_blocks + 4, total_rows // BLK), clear, 0)

    def joined(ref, b):
        return jnp.concatenate(
            [
                ref[pl.ds(4 * b, 1), :] + ref[pl.ds(4 * b + 1, 1), :],
                ref[pl.ds(4 * b + 2, 1), :] + ref[pl.ds(4 * b + 3, 1), :],
            ],
            axis=1,
        )

    code_rows = iota((CODES, 256), 0)
    which = lax.broadcasted_iota(jnp.int32, (128, 256), 0)

    def compact(b, p):
        x4 = x_ref[pl.ds(4 * b, 4)].astype(F32)
        xcat = jnp.concatenate([x4[:, i * slots : i * slots + 64].reshape(256, 128) for i in range(3)], axis=1).astype(BF16)
        row = joined(code, b) - jnp.asarray(p * CODES + 1, F32)
        where_at = jnp.where(which == 0, joined(high, b) * 256.0, jnp.where(which == 1, joined(low, b), 0.0)).astype(BF16)
        select = jnp.where(code_rows == row, 1.0, 0.0).astype(BF16)
        y = jnp.concatenate([dot(select, xcat), nt_dot(select, where_at)], axis=1).astype(BF16)
        ats = [pl.ds(pl.multiple_of(tab[4 * b, c] + p * RUN, 16), RUN) for c in range(CL_SET)]
        new = [xs[at, :] + y[c * RUN : (c + 1) * RUN] for c, at in enumerate(ats)]
        for at, x in zip(ats, new):
            xs[at, :] = x

    def each_block(body):
        def some(i, _):
            for u in range(UNROLL):
                body(i * UNROLL + u, 0)
            return 0

        lax.fori_loop(0, blocks // UNROLL, some, 0)

        @pl.when(tab[0, 10] > 1)
        def _():
            def rest(b, _):
                def more(p, _):
                    body(b, p)
                    return 0

                return lax.fori_loop(1, tab[4 * b, 8], more, 0)

            lax.fori_loop(0, blocks, rest, 0)

    each_block(compact)

    scale = HEAD_DIM ** (-0.5) * 1.4426950408889634
    to_lanes = jnp.where(lax.broadcasted_iota(jnp.int32, (16, 128), 1) < 2, 1.0, 0.0).astype(BF16)
    to_all = jnp.where(lax.broadcasted_iota(jnp.int32, (128, 128), 0) < 2, 1.0, 0.0).astype(BF16)

    def key_places(at):
        kp = nt_dot(to_lanes, xs[at, 384:512])[0:1]
        return jnp.where(kp > 0.0, kp, 1e9)

    def hidden(scores, kp, qp):
        lanes = scores.shape[1] // 128
        return jnp.where(kp <= jnp.concatenate([qp] * lanes, axis=1), scores * scale, HIDDEN)

    def fixed(begin, count):
        kat = pl.ds(pl.multiple_of(begin * BLK, BLK), count * BLK)
        keys = xs[kat, 128:256]
        values = xs[kat, 256:384]
        kp = key_places(kat)
        for i in range(0, count, 2):
            wide = min(2, count - i)
            at = pl.ds(pl.multiple_of((begin + i) * BLK, BLK), wide * BLK)
            scores = hidden(nt_dot(xs[at, 0:128], keys), kp, dot(xs[at, 384:512], to_all))
            weight = jnp.exp2(scores - jnp.max(scores, axis=1, keepdims=True))
            total = jnp.sum(weight, axis=1, keepdims=True)
            os[at, :] = (dot(weight.astype(BF16), values) / total).astype(BF16)

    def general(begin, count):
        def queries(i, _):
            at = pl.ds(pl.multiple_of((begin + i) * BLK, BLK), BLK)
            q = xs[at, 0:128]
            qp = dot(xs[at, 384:512], to_all)

            def keys(j, carried):
                top, total, summed = carried
                kat = pl.ds(pl.multiple_of((begin + j) * BLK, BLK), BLK)
                scores = hidden(nt_dot(q, xs[kat, 128:256]), key_places(kat), qp)
                fresh = jnp.maximum(top, jnp.max(scores, axis=1, keepdims=True))
                weight = jnp.exp2(scores - fresh)
                rescale = jnp.exp2(top - fresh)
                total = total * rescale + jnp.sum(weight, axis=1, keepdims=True)
                summed = summed * rescale + dot(weight.astype(BF16), xs[kat, 256:384])
                return fresh, total, summed

            init = (jnp.full((BLK, 1), HIDDEN, F32), jnp.zeros((BLK, 1), F32), jnp.zeros((BLK, 128), F32))
            _, total, summed = lax.fori_loop(0, count, keys, init)
            os[at, :] = (summed / total).astype(BF16)
            return 0

        lax.fori_loop(0, count, queries, 0)

    def cluster(c, _):
        begin = tab[0, 16 + c]
        count = tab[0, 24 + c]
        for n in FIXED:
            pl.when(count == n)(functools.partial(fixed, begin, n))
        pl.when((count < FIXED[0]) | (count > FIXED[-1]))(functools.partial(general, begin, count))
        return 0

    lax.fori_loop(0, CL_SET, cluster, 0)

    code_lanes = iota((256, CODES), 1)

    def spread(b, p):
        col = column(joined(code, b) - jnp.asarray(p * CODES + 1, F32))
        col = jnp.concatenate([col] * (CODES // 128), axis=1)
        cat = jnp.concatenate(
            [os[pl.ds(pl.multiple_of(tab[4 * b, c] + p * RUN, 16), RUN), :] for c in range(CL_SET)], axis=0
        )
        select = jnp.where(code_lanes == col, 1.0, 0.0).astype(BF16)
        new = dot(select, cat).reshape(4, 64, 128)[:, :slots]
        at = pl.ds(4 * b, 4)
        if isinstance(p, int):
            o_ref[at] = new.astype(BF16)
        else:
            o_ref[at] = (o_ref[at].astype(F32) + new).astype(BF16)

    each_block(spread)


def attend_call(slots, got):
    sources = got.shape[0]
    whole = pl.BlockSpec(memory_space=pltpu.VMEM)
    total_rows = sources * slots + (CL_SET + 4) * BLK
    return pl.pallas_call(
        functools.partial(attend_kernel, slots),
        in_specs=[whole],
        out_specs=whole,
        out_shape=jax.ShapeDtypeStruct((sources, slots, 128), BF16),
        scratch_shapes=[
            pltpu.VMEM((total_rows, 4 * HEAD_DIM), BF16),
            pltpu.VMEM((total_rows, HEAD_DIM), BF16),
            pltpu.VMEM((sources, 128), F32),
            pltpu.VMEM((sources, 128), F32),
            pltpu.VMEM((sources, 128), F32),
            pltpu.VMEM((sources, 128), jnp.int32),
            pltpu.SMEM((sources, 128), jnp.int32),
            pltpu.SemaphoreType.DMA,
        ],
        compiler_params=pltpu.CompilerParams(vmem_limit_bytes=56 * 2**20),
        name="attend",
    )(got)


def unpack_kernel(slots, slot_ref, r_ref, out_ref, select):
    sets, heads = r_ref.shape[0], r_ref.shape[1]

    @pl.when(pl.program_id(0) == 0)
    def _():
        col = column(slot_ref[...])
        col = jnp.concatenate([col] * (-(-sets * slots // 128)), axis=1)[:, : sets * slots]
        select[...] = jnp.where(iota(select.shape, 1) == col, 1.0, 0.0).astype(BF16)

    for h in range(heads):
        x = r_ref[:, h].astype(F32).reshape(sets * slots, 128).astype(BF16)
        out_ref[:, h * 128 : (h + 1) * 128] = dot(select[...], x).astype(BF16)


def pack_call(slots, sets, parity, cid_row, pos_row, queries, keys, values):
    tokens, width = queries.shape
    heads = width // HEAD_DIM
    rows = chunk_rows(slots)
    some = pl.BlockSpec((tokens, PACK * HEAD_DIM), lambda h: (0, h))
    line = pl.BlockSpec((1, tokens), lambda h: (0, 0))
    return pl.pallas_call(
        functools.partial(pack_kernel, slots, sets),
        grid=(heads // PACK,),
        in_specs=[pl.BlockSpec(memory_space=pltpu.SMEM), line, line, some, some, some],
        out_specs=[pl.BlockSpec((sets, PACK, rows, 128), lambda h: (0, h, 0, 0)), line],
        out_shape=[
            jax.ShapeDtypeStruct((sets, heads, rows, 128), BF16),
            jax.ShapeDtypeStruct((1, tokens), F32),
        ],
        scratch_shapes=[pltpu.VMEM((sets * slots, tokens), BF16), pltpu.VMEM((16, sets * 128), F32)],
        compiler_params=pltpu.CompilerParams(vmem_limit_bytes=56 * 2**20),
        name="pack",
    )(parity, cid_row, pos_row, queries, keys, values)


def unpack_call(slots, slot, back):
    sets, heads = back.shape[:2]
    tokens = slot.shape[1]
    return pl.pallas_call(
        functools.partial(unpack_kernel, slots),
        grid=(heads // UNPACK,),
        in_specs=[
            pl.BlockSpec((1, tokens), lambda h: (0, 0)),
            pl.BlockSpec((sets, UNPACK, slots, 128), lambda h: (0, h, 0, 0)),
        ],
        out_specs=pl.BlockSpec((tokens, UNPACK * HEAD_DIM), lambda h: (0, h)),
        out_shape=jax.ShapeDtypeStruct((tokens, heads * HEAD_DIM), BF16),
        scratch_shapes=[pltpu.VMEM((tokens, sets * slots), BF16)],
        compiler_params=pltpu.CompilerParams(vmem_limit_bytes=56 * 2**20),
        name="unpack",
    )(slot, back)


def attention(slots, queries, keys, values, cid_row, pos_row, parity):
    heads = queries.shape[1] // HEAD_DIM
    sources = lax.axis_size("grp") * lax.axis_size("blk")
    sets = sources // heads
    sent, slot = pack_call(slots, sets, parity, cid_row, pos_row, queries, keys, values)
    got = lax.all_to_all(
        sent.reshape(sources, sent.shape[2], 128), ("grp", "blk"), split_axis=0, concat_axis=0, tiled=True
    )
    done = attend_call(slots, got)
    back = lax.all_to_all(done, ("grp", "blk"), split_axis=0, concat_axis=0, tiled=True)
    return unpack_call(slots, slot, back.reshape(sets, heads, slots, 128))


def local(queries, keys, values, cluster_ids, positions):
    cid_row = cluster_ids.reshape(1, -1)
    pos_row = positions.reshape(1, -1)
    me = lax.axis_index("grp") * lax.axis_size("blk") + lax.axis_index("blk")
    parity = (me % 2).astype(jnp.int32).reshape(1, 1)
    return attention(2 * 32, queries, keys, values, cid_row, pos_row, parity)


def solution(mesh):
    placed = (
        P(("grp", "blk"), None),
        P(("grp", "blk"), None),
        P(("grp", "blk"), None),
        P(("grp", "blk")),
        P(("grp", "blk")),
    )
    return jax.shard_map(
        local, mesh=mesh, in_specs=placed, out_specs=P(("grp", "blk"), None), check_vma=False
    )
```

time: 218 us -> 166 us (0.76)
  Pallas kernels: 77.2 us -> 38 us
  blocking collectives: 141 us -> 128 us
    pallas_call x3, Pallas kernels: 77.2 us -> 38 us  [the longest x1 28.2 us: attend_call(): pl.pallas_call(functools.partial(attend_kernel, slots), in_specs=[whole],...]
    all_to_all x1, blocking collectives: 49.3 us -> 36.3 us  [attention(): lax.all_to_all(done, ('grp', 'blk'), split_axis=0, concat_axis=0, tiled=T...]
where the time goes in v2:
time: 166 us
  blocking collectives  128 us (77%)
  Pallas kernels  38 us (23%)
    all_to_all x1, blocking collectives, attention(): lax.all_to_all(sent.reshape(sources, sent.shape[2], 128), ('grp', 'blk'),...  91.4 us
    all_to_all x1, blocking collectives, attention(): lax.all_to_all(done, ('grp', 'blk'), split_axis=0, concat_axis=0, tiled=T...  36.3 us
    pallas_call x1, Pallas kernels, attend_call(): pl.pallas_call(functools.partial(attend_kernel, slots), in_specs=[whole],...  28.2 us
    pallas_call x1, Pallas kernels, pack_call(): pl.pallas_call(functools.partial(pack_kernel, slots, sets), grid=(heads /...  6.19 us
    pallas_call x1, Pallas kernels, unpack_call(): pl.pallas_call(functools.partial(unpack_kernel, slots), grid=(heads // UN...  3.54 us

profile of v2, /device:TPU:0, one launch (start us, length us, event | category | flops | bytes accessed | tf_op | source)
XLA Modules:
  0.0 165.7 jit_solution(3340344600974224423)
XLA Ops:
  0.0 6.2 %pack.1 = (bf16[8,16,208,128]{3,2,1,0:T(8,128)(2,1)}, f32[1,256]{1,0:T(1,128)}) custom-call(s32[1,1]{1,0:T(1,128)} %bitcast.parity_ref, s32[1,256]{1,0:T(1,128)} %bitcast.7, s32[1,256]{1,0:T(1,128)} %bitcast.8, bf16[256,2048]{1,0:T(8,128)(2,1)} %q_ref.1, bf16[256,2048]{1,0:T(8,128)(2,1)} %k_ref.1, bf16[256,2048]{1,0:T(8,128)(2,1)} %v_ref.1), custom_call_target="tpu_custom_call" | custom-call | tf_op jit(solution)/shard_map/pack/pallas_call | solution.py:318
  6.2 91.4 %all_to_all.10.x_ref = bf16[128,208,128]{2,1,0:T(8,128)(2,1)} all-to-all(bf16[128,208,128]{2,1,0:T(8,128)(2,1)} %bitcast.6), channel_id=1, replica_groups=mesh['grp'=16,'blk'=8] {'grp','blk'}, dimensions={0} | all-to-all | bytes 13631488 | tf_op jit(solution)/shard_map/all_to_all | solution.py:356
  97.6 28.2 %attend.1 = bf16[128,64,128]{2,1,0:T(8,128)(2,1)} custom-call(bf16[128,208,128]{2,1,0:T(8,128)(2,1)} %all_to_all.10.x_ref), custom_call_target="tpu_custom_call" | custom-call | tf_op jit(solution)/shard_map/attend/pallas_call | solution.py:278
  125.8 36.3 %all_to_all.11 = bf16[128,64,128]{2,1,0:T(8,128)(2,1)} all-to-all(bf16[128,64,128]{2,1,0:T(8,128)(2,1)} %attend.1), channel_id=1, replica_groups=mesh['grp'=16,'blk'=8] {'grp','blk'}, dimensions={0} | all-to-all | bytes 4194304 | tf_op jit(solution)/shard_map/all_to_all | solution.py:360
  162.2 3.5 %unpack.1 = bf16[256,2048]{1,0:T(8,128)(2,1)} custom-call(f32[1,256]{1,0:T(1,128)} %get-tuple-element.7.slot_ref, bf16[8,16,64,128]{3,2,1,0:T(8,128)(2,1)} %bitcast.5), custom_call_target="tpu_custom_call" | custom-call | tf_op jit(solution)/shard_map/unpack/pallas_call | solution.py:336

commit v3 on v2

--- a/solution.py
+++ b/solution.py
@@ -15,6 +15,8 @@
 BLK = 128
 FIXED = (4, 5, 6)
 UNROLL = 8
+ALL = 64
+FEW = 56
 PACK = 8
 UNPACK = 8
 F32 = jnp.float32
@@ -63,6 +65,7 @@
         place[...] = jnp.where(iota((sets * slots, tokens), 0) == slot, 1.0, 0.0).astype(BF16)
         lane = jnp.where(fits, group * 128 + rank + 64 * parity_ref[0, 0].astype(F32), -1.0)
         spread = jnp.where(iota((sets * 128, tokens), 0) == lane, 1.0, 0.0).astype(BF16)
+        short = jnp.where(jnp.max(rank, axis=1, keepdims=True) >= slots, 1.0, 0.0)
         low = jnp.bitwise_and(pos, 255)
         high = jnp.right_shift(pos, 8) + 1
         row = lax.broadcasted_iota(jnp.int32, (16, tokens), 0)
@@ -72,6 +75,7 @@
             jnp.where(row == 1, low.astype(F32), jnp.where(row == 2, own.astype(F32) + 1.0, jnp.where(row == 3, within, 0.0))),
         ).astype(BF16)
         meta[...] = nt_dot(facts, spread)
+        meta[4:5, :] = jnp.broadcast_to(short, (1, sets * 128))
 
     gap = out_ref.shape[2] - 3 * slots - 8
     for h in range(out_ref.shape[1]):
@@ -86,7 +90,7 @@
             out_ref[s, h] = jnp.concatenate(pieces, axis=0).astype(BF16)
 
 
-def attend_kernel(slots, x_ref, o_ref, xs, os, code, high, low, tab_v, tab, sem):
+def attend_kernel(slots, x_ref, o_ref, short_ref, xs, os, code, high, low, tab_v, tab, sem):
     sources, rows, _ = x_ref.shape
     blocks = sources // 4
     total_rows = xs.shape[0]
@@ -96,6 +100,7 @@
     low[...] = facts[:, 9, :]
     own = facts[:, 10, :]
     within = facts[:, 11, :]
+    short_ref[...] = jnp.broadcast_to(jnp.max(facts[:, 12, :], axis=0, keepdims=True), (8, 128))
     lane = iota((sources, 128), 1)
     counts = jnp.zeros((sources, 128), F32)
     for c in range(CL_SET):
@@ -278,8 +283,11 @@
     return pl.pallas_call(
         functools.partial(attend_kernel, slots),
         in_specs=[whole],
-        out_specs=whole,
-        out_shape=jax.ShapeDtypeStruct((sources, slots, 128), BF16),
+        out_specs=[whole, whole],
+        out_shape=[
+            jax.ShapeDtypeStruct((sources, slots, 128), BF16),
+            jax.ShapeDtypeStruct((8, 128), F32),
+        ],
         scratch_shapes=[
             pltpu.VMEM((total_rows, 4 * HEAD_DIM), BF16),
             pltpu.VMEM((total_rows, HEAD_DIM), BF16),
@@ -348,7 +356,7 @@
     )(slot, back)
 
 
-def attention(slots, queries, keys, values, cid_row, pos_row, parity):
+def attention(slots, queries, keys, values, cid_row, pos_row, parity, fallback=None):
     heads = queries.shape[1] // HEAD_DIM
     sources = lax.axis_size("grp") * lax.axis_size("blk")
     sets = sources // heads
@@ -356,9 +364,12 @@
     got = lax.all_to_all(
         sent.reshape(sources, sent.shape[2], 128), ("grp", "blk"), split_axis=0, concat_axis=0, tiled=True
     )
-    done = attend_call(slots, got)
+    done, short = attend_call(slots, got)
     back = lax.all_to_all(done, ("grp", "blk"), split_axis=0, concat_axis=0, tiled=True)
-    return unpack_call(slots, slot, back.reshape(sets, heads, slots, 128))
+    back = back.reshape(sets, heads, slots, 128)
+    if fallback is None:
+        return unpack_call(slots, slot, back)
+    return lax.cond(short[0, 0] > 0.0, fallback, lambda: unpack_call(slots, slot, back))
 
 
 def local(queries, keys, values, cluster_ids, positions):
@@ -366,7 +377,8 @@
     pos_row = positions.reshape(1, -1)
     me = lax.axis_index("grp") * lax.axis_size("blk") + lax.axis_index("blk")
     parity = (me % 2).astype(jnp.int32).reshape(1, 1)
-    return attention(2 * 32, queries, keys, values, cid_row, pos_row, parity)
+    args = (queries, keys, values, cid_row, pos_row, parity)
+    return attention(FEW, *args, fallback=lambda: attention(ALL, *args))
 
 
 def solution(mesh):

time: 166 us -> 149 us (0.90)
  blocking collectives: 128 us -> 79.8 us
  waiting for transfers between devices: 0 us -> 24.9 us
  starting transfers between devices: 0 us -> 7.2 us
  Pallas kernels: 38 us -> 33.5 us
  local copies, waits for them, and re-layouts: 0 us -> 2.2 us
    all_to_all x1 -> x0, blocking collectives: 36.3 us -> none  [attention(): lax.all_to_all(done, ('grp', 'blk'), split_axis=0, concat_axis=0, tiled=T...]
    all_to_all x0 -> x1, waiting for transfers between devices: none -> 24.9 us  [attention(): lax.all_to_all(done, ('grp', 'blk'), split_axis=0, concat_axis=0, tiled=T...]
    all_to_all x1, blocking collectives: 91.4 us -> 79.8 us  [attention(): lax.all_to_all(sent.reshape(sources, sent.shape[2], 128), ('grp', 'blk'),...]
    all_to_all x0 -> x1, starting transfers between devices: none -> 7.2 us  [attention(): lax.all_to_all(done, ('grp', 'blk'), split_axis=0, concat_axis=0, tiled=T...]
    pallas_call x1, Pallas kernels: 28.2 us -> 26 us  [attend_call(): pl.pallas_call(functools.partial(attend_kernel, slots), in_specs=[whole],...]
    pallas_call x1, Pallas kernels: 3.54 us -> 1.73 us  [unpack_call(): pl.pallas_call(functools.partial(unpack_kernel, slots), grid=(heads // UN...]
  transfers between devices with their start and end apart: 0 -> 1, of which waited for: 0 -> 1; matrix products, arithmetic and copies ran while one was open for 0% -> 1% of each run, Pallas kernels for 0% -> 0%
where the time goes in v3:
time: 149 us
  blocking collectives  79.8 us (54%)
  Pallas kernels  33.5 us (22%)
  waiting for transfers between devices  24.9 us (17%)
  starting transfers between devices  7.2 us (5%)
  local copies, waits for them, and re-layouts  2.2 us (1%)
    all_to_all x1, blocking collectives, attention(): lax.all_to_all(sent.reshape(sources, sent.shape[2], 128), ('grp', 'blk'),...  79.8 us
    pallas_call x1, Pallas kernels, attend_call(): pl.pallas_call(functools.partial(attend_kernel, slots), in_specs=[whole],...  26 us
    all_to_all x1, waiting for transfers between devices, attention(): lax.all_to_all(done, ('grp', 'blk'), split_axis=0, concat_axis=0, tiled=T...  24.9 us
    all_to_all x1, starting transfers between devices, attention(): lax.all_to_all(done, ('grp', 'blk'), split_axis=0, concat_axis=0, tiled=T...  7.2 us
    pallas_call x1, Pallas kernels, pack_call(): pl.pallas_call(functools.partial(pack_kernel, slots, sets), grid=(heads /...  5.75 us
  transfers between devices with their start and end apart: 1, of which 1 were waited for; matrix products, arithmetic and copies ran while one was open for 1% of the time, Pallas kernels for 0%

profile of v3, /device:TPU:0, one launch (start us, length us, event | category | flops | bytes accessed | tf_op | source)
XLA Modules:
  0.0 148.6 jit_solution(5625396322456290905)
XLA Ops:
  0.0 5.8 %pack.3 = (bf16[8,16,176,128]{3,2,1,0:T(8,128)(2,1)}, f32[1,256]{1,0:T(1,128)S(1)}) custom-call(s32[1,1]{1,0:T(1,128)} %bitcast.3.parity_ref, s32[1,256]{1,0:T(1,128)} %bitcast.12, s32[1,256]{1,0:T(1,128)} %bitcast.14, bf16[256,2048]{1,0:T(8,128)(2,1)} %q_ref.1, bf16[256,2048]{1,0:T(8,128)(2,1)} %k_ref.1, bf16[256,2048]{1,0:T(8,128)(2,1)} %v_ref.1), custom_call_target="tpu_custom_call" | custom-call | tf_op jit(solution)/shard_map/pack/pallas_call | solution.py:326
  5.8 79.8 %all_to_all.20.x_ref = bf16[128,176,128]{2,1,0:T(8,128)(2,1)} all-to-all(bf16[128,176,128]{2,1,0:T(8,128)(2,1)} %bitcast.11), channel_id=1, replica_groups=mesh['grp'=16,'blk'=8] {'grp','blk'}, dimensions={0} | all-to-all | bytes 11534336 | tf_op jit(solution)/shard_map/all_to_all | solution.py:364
  85.6 0.0 copy-start
  85.6 0.0 copy-start.2
  85.6 0.0 copy-start.3
  85.6 26.0 %attend.3 = (bf16[128,56,128]{2,1,0:T(8,128)(2,1)}, f32[8,128]{1,0:T(8,128)}) custom-call(bf16[128,176,128]{2,1,0:T(8,128)(2,1)} %all_to_all.20.x_ref), custom_call_target="tpu_custom_call" | custom-call | tf_op jit(solution)/shard_map/attend/pallas_call | solution.py:283
  111.6 7.2 %all-to-all-start.3 = ((bf16[128,56,128]{2,1,0:T(8,128)(2,1)}), bf16[128,56,128]{2,1,0:T(8,128)(2,1)S(1)}, u32[]{:S(2)}, u32[]{:S(2)}) async-start(bf16[128,56,128]{2,1,0:T(8,128)(2,1)} %get-tuple-element.42), calls=%async_computation.3 | async-start | bytes 3670016 | tf_op jit(solution)/shard_map/all_to_all | solution.py:368
  118.8 1.2 slice.3
  120.7 24.9 %all-to-all-done.3 = bf16[128,56,128]{2,1,0:T(8,128)(2,1)S(1)} async-done(((bf16[128,56,128]{2,1,0:T(8,128)(2,1)}), bf16[128,56,128]{2,1,0:T(8,128)(2,1)S(1)}, u32[]{:S(2)}, u32[]{:S(2)}) %all-to-all-start.3) | async-done | bytes 1835040 | tf_op jit(solution)/shard_map/all_to_all | solution.py:368
  145.6 0.0 copy-done
  145.6 0.0 copy-done.2
  145.6 0.0 copy-done.3
  145.6 2.0 %conditional.1 = (bf16[256,2048]{1,0:T(8,128)(2,1)S(1)}) conditional(s32[]{:T(128)} %bitcast.7, (bf16[128,56,128]{2,1,0:T(8,128)(2,1)S(1)}, f32[1,256]{1,0:T(1,128)S(1)}) %tuple.11, (s32[1,1]{1,0:T(1,128)}, s32[1,256]{1,0:T(1,128)S(1)}, s32[1,256]{1,0:T(1,128)S(1)}, bf16[256,2048]{1,0:T(8,128)(2,1)S(1)}, bf16[256,2048]{1,0:T(8,128)(2,1)}, ...), branch_computations={%region_0.1_spmd, %region_1.2_spmd} | conditional | bytes 17825800 | solution.py:372
  145.6 1.7 %unpack.2 = bf16[256,2048]{1,0:T(8,128)(2,1)S(1)} custom-call(f32[1,256]{1,0:T(1,128)S(1)} %get-tuple-element.25.slot_ref, bf16[8,16,56,128]{3,2,1,0:T(8,128)(2,1)S(1)} %bitcast.9), custom_call_target="tpu_custom_call" | custom-call | tf_op jit(solution)/shard_map/cond/branch_0_fun/unpack/pallas_call | solution.py:344
  147.6 0.0 copy-start.1
  147.6 1.0 copy-done.1
Async XLA Ops:
  85.6 60.0 %copy-start = (bf16[256,2048]{1,0:T(8,128)(2,1)S(1)}, bf16[256,2048]{1,0:T(8,128)(2,1)}, u32[]{:S(2)}) copy-start(bf16[256,2048]{1,0:T(8,128)(2,1)} %q_ref.1) | copy-start | bytes 3145732
  85.6 60.0 %copy-start.2 = (s32[256]{0:T(256)S(1)}, s32[256]{0:T(256)}, u32[]{:S(2)}) copy-start(s32[256]{0:T(256)} %param.10) | copy-start | bytes 3076
  85.6 60.0 %copy-start.3 = (s32[256]{0:T(256)S(1)}, s32[256]{0:T(256)}, u32[]{:S(2)}) copy-start(s32[256]{0:T(256)} %param.11) | copy-start | bytes 3076
  111.6 34.0 %all-to-all-start.3 = ((bf16[128,56,128]{2,1,0:T(8,128)(2,1)}), bf16[128,56,128]{2,1,0:T(8,128)(2,1)S(1)}, u32[]{:S(2)}, u32[]{:S(2)}) async-start(bf16[128,56,128]{2,1,0:T(8,128)(2,1)} %get-tuple-element.42), calls=%async_computation.3 | async-start | bytes 3670016 | tf_op jit(solution)/shard_map/all_to_all | solution.py:368
  147.6 1.0 copy-start.1

commit v4 on v3

--- a/solution.py
+++ b/solution.py
@@ -15,6 +15,8 @@
 BLK = 128
 FIXED = (4, 5, 6)
 UNROLL = 8
+TILE = 3
+JOINT = 2
 ALL = 64
 FEW = 56
 PACK = 8
@@ -90,68 +92,86 @@
             out_ref[s, h] = jnp.concatenate(pieces, axis=0).astype(BF16)
 
 
-def attend_kernel(slots, x_ref, o_ref, short_ref, xs, os, code, high, low, tab_v, tab, sem):
+def attend_kernel(
+    slots, x_hbm, o_hbm, short_ref, x_ref, o_ref, facts_ref, flat, xs, os, code, high, low, tab_v, tab, sem, facts_sem, in_sems, out_sems
+):
     sources, rows, _ = x_ref.shape
-    blocks = sources // 4
+    step_rows = 4 * UNROLL
+    steps = sources // step_rows
+    facts_in = pltpu.make_async_copy(x_hbm.at[:, rows - 16 : rows, :], facts_ref, facts_sem)
+    facts_in.start()
+
+    def part_in(i):
+        at = pl.ds(i * step_rows, step_rows)
+        return pltpu.make_async_copy(x_hbm.at[at], x_ref.at[at], in_sems.at[i])
+
+    def part_out(i):
+        at = pl.ds(i * step_rows, step_rows)
+        return pltpu.make_async_copy(o_ref.at[at], o_hbm.at[at], out_sems.at[i])
+
+    for i in range(steps):
+        part_in(i).start()
+    os[...] = jnp.zeros(os.shape, BF16)
+    ahead = 5 * sources // 16
+    xs[0 : ahead * BLK, :] = jnp.zeros((ahead * BLK, xs.shape[1]), BF16)
+    facts_in.wait()
     total_rows = xs.shape[0]
 
-    facts = x_ref[:, rows - 16 : rows, :].astype(F32)
-    high[...] = facts[:, 8, :]
-    low[...] = facts[:, 9, :]
-    own = facts[:, 10, :]
-    within = facts[:, 11, :]
-    short_ref[...] = jnp.broadcast_to(jnp.max(facts[:, 12, :], axis=0, keepdims=True), (8, 128))
+    flat[...] = facts_ref[...].astype(F32)[:, 8:16].reshape(flat.shape)
+
+    def fact(i):
+        return flat[pl.ds(i, sources, 8), :]
+
+    high[...] = fact(0) * 256.0
+    low[...] = fact(1)
+    own = fact(2)
+    within = fact(3)
+    short_ref[...] = jnp.broadcast_to(jnp.max(fact(4), axis=0, keepdims=True), (8, 128))
     lane = iota((sources, 128), 1)
-    counts = jnp.zeros((sources, 128), F32)
-    for c in range(CL_SET):
-        n = jnp.sum(jnp.where(own == c + 1, 1.0, 0.0), axis=1, keepdims=True)
-        counts = counts + jnp.where(lane == c, n, 0.0)
-    counts16 = counts.astype(BF16)
+    r = lax.broadcasted_iota(jnp.int32, (128, CL_SET * 128), 0)
+    s = lax.broadcasted_iota(jnp.int32, (128, CL_SET * 128), 1)
+    to_each = jnp.where(r == jnp.right_shift(s, 7), 1.0, 0.0).astype(BF16)
+    is_own = [jnp.where(own == c + 1, 1.0, 0.0) for c in range(CL_SET)]
+    counts = nt_dot(jnp.concatenate(is_own, axis=1).astype(BF16), to_each).astype(BF16)
     r = lax.broadcasted_iota(jnp.int32, (sources, sources), 0)
     s = lax.broadcasted_iota(jnp.int32, (sources, sources), 1)
-
-    def picked(mask):
-        return dot(jnp.where(mask, 1.0, 0.0).astype(BF16), counts16)
-
     first = jnp.bitwise_and(r, -4)
-    before = picked(s < r)
-    before_block = picked(s < first)
-    after_block = picked(s < first + 4)
-    total = picked(s >= 0)
+    masks = [s >= 0, s < r, s < first, s < first + 4]
+    sums = dot(jnp.concatenate([jnp.where(m, 1.0, 0.0) for m in masks], axis=0).astype(BF16), counts)
+    total, before, before_block, after_block = (sums[i * sources : (i + 1) * sources] for i in range(4))
     nblk = jnp.floor((total + (BLK - 1)) * (1.0 / BLK))
     start_blk = dot(nblk.astype(BF16), jnp.where((r < s) & (r < CL_SET), 1.0, 0.0).astype(BF16))
-    base = start_blk * BLK
-    aligned = base + jnp.floor(before_block * (1.0 / 16)) * 16
-    shift = base + before - aligned
-    passes = jnp.where(lane < CL_SET, jnp.floor((base + after_block - aligned + (RUN - 1)) * (1.0 / RUN)), 0.0)
-    passes = jnp.max(passes, axis=1, keepdims=True)
+    skipped = jnp.floor(before_block * (1.0 / 16)) * 16
+    shift = dot((before - skipped).astype(BF16), to_each)
     place = within
     for c in range(CL_SET):
-        place = place + jnp.where(own == c + 1, shift[:, c : c + 1], 0.0)
+        place = place + is_own[c] * shift[:, c * 128 : (c + 1) * 128]
     step = jnp.floor(place * (1.0 / RUN) + (0.5 / RUN))
     code[...] = jnp.where(own > 0.0, step * CODES + (own - 1.0) * RUN + (place - step * RUN) + 1.0, 0.0)
-    last = start_blk + nblk
-    used = jnp.max(jnp.where(lane < CL_SET, last, 0.0), axis=1, keepdims=True)
-    table = jnp.where(lane < CL_SET, aligned, 0.0)
-    table = jnp.where(lane == 8, passes, table)
-    table = jnp.where(lane == 9, used, table)
-    table = jnp.where(lane == 10, jnp.max(passes), table)
-    spin = jnp.zeros((sources, 128), F32)
-    for c in range(CL_SET):
-        spin = spin + jnp.where(lane == 16 + c, start_blk[:, c : c + 1], 0.0) + jnp.where(lane == 24 + c, nblk[:, c : c + 1], 0.0)
-    tab_v[...] = (table + spin).astype(jnp.int32)
+    passes = jnp.max(jnp.where(lane < CL_SET, after_block - skipped, 0.0), axis=(0, 1), keepdims=True)
+    passes = jnp.floor((passes + (RUN - 1)) * (1.0 / RUN))
+    tab_v[0:sources] = jnp.where(lane < CL_SET, start_blk * BLK + skipped, passes).astype(jnp.int32)
+    tab_v[sources : sources + 8] = start_blk[0:8].astype(jnp.int32)
+    tab_v[sources + 8 : sources + 16] = nblk[0:8].astype(jnp.int32)
     copy = pltpu.make_async_copy(tab_v, tab, sem)
     copy.start()
-    os[...] = jnp.zeros(os.shape, BF16)
     copy.wait()
-    used_blocks = tab[0, 9]
+    most_passes = tab[0, CL_SET]
+
+    def begin_of(c):
+        return tab[sources, c]
+
+    def count_of(c):
+        return tab[sources + 8, c]
+
+    used_blocks = begin_of(CL_SET - 1) + count_of(CL_SET - 1)
 
     def clear(i, _):
         at = pl.ds(pl.multiple_of(i * BLK, BLK), BLK)
         xs[at, :] = jnp.zeros((BLK, xs.shape[1]), BF16)
         return 0
 
-    lax.fori_loop(0, jnp.minimum(used_blocks + 4, total_rows // BLK), clear, 0)
+    lax.fori_loop(ahead, jnp.minimum(used_blocks + 4, total_rows // BLK), clear, 0)
 
     def joined(ref, b):
         return jnp.concatenate(
@@ -169,7 +189,7 @@
         x4 = x_ref[pl.ds(4 * b, 4)].astype(F32)
         xcat = jnp.concatenate([x4[:, i * slots : i * slots + 64].reshape(256, 128) for i in range(3)], axis=1).astype(BF16)
         row = joined(code, b) - jnp.asarray(p * CODES + 1, F32)
-        where_at = jnp.where(which == 0, joined(high, b) * 256.0, jnp.where(which == 1, joined(low, b), 0.0)).astype(BF16)
+        where_at = jnp.where(which == 0, joined(high, b), jnp.where(which == 1, joined(low, b), 0.0)).astype(BF16)
         select = jnp.where(code_rows == row, 1.0, 0.0).astype(BF16)
         y = jnp.concatenate([dot(select, xcat), nt_dot(select, where_at)], axis=1).astype(BF16)
         ats = [pl.ds(pl.multiple_of(tab[4 * b, c] + p * RUN, 16), RUN) for c in range(CL_SET)]
@@ -177,26 +197,33 @@
         for at, x in zip(ats, new):
             xs[at, :] = x
 
-    def each_block(body):
+    def each_block(body, before=None, after=None):
         def some(i, _):
+            if before is not None:
+                before(i)
             for u in range(UNROLL):
                 body(i * UNROLL + u, 0)
+
+            @pl.when(most_passes > 1)
+            def _():
+                def rest(u, _):
+                    b = i * UNROLL + u
+
+                    def more(p, _):
+                        body(b, p)
+                        return 0
+
+                    return lax.fori_loop(1, most_passes, more, 0)
+
+                lax.fori_loop(0, UNROLL, rest, 0)
+
+            if after is not None:
+                after(i)
             return 0
 
-        lax.fori_loop(0, blocks // UNROLL, some, 0)
-
-        @pl.when(tab[0, 10] > 1)
-        def _():
-            def rest(b, _):
-                def more(p, _):
-                    body(b, p)
-                    return 0
-
-                return lax.fori_loop(1, tab[4 * b, 8], more, 0)
-
-            lax.fori_loop(0, blocks, rest, 0)
-
-    each_block(compact)
+        lax.fori_loop(0, steps, some, 0)
+
+    each_block(compact, before=lambda i: part_in(i).wait())
 
     scale = HEAD_DIM ** (-0.5) * 1.4426950408889634
     to_lanes = jnp.where(lax.broadcasted_iota(jnp.int32, (16, 128), 1) < 2, 1.0, 0.0).astype(BF16)
@@ -210,18 +237,21 @@
         lanes = scores.shape[1] // 128
         return jnp.where(kp <= jnp.concatenate([qp] * lanes, axis=1), scores * scale, HIDDEN)
 
-    def fixed(begin, count):
-        kat = pl.ds(pl.multiple_of(begin * BLK, BLK), count * BLK)
-        keys = xs[kat, 128:256]
-        values = xs[kat, 256:384]
-        kp = key_places(kat)
-        for i in range(0, count, 2):
-            wide = min(2, count - i)
-            at = pl.ds(pl.multiple_of((begin + i) * BLK, BLK), wide * BLK)
-            scores = hidden(nt_dot(xs[at, 0:128], keys), kp, dot(xs[at, 384:512], to_all))
-            weight = jnp.exp2(scores - jnp.max(scores, axis=1, keepdims=True))
-            total = jnp.sum(weight, axis=1, keepdims=True)
-            os[at, :] = (dot(weight.astype(BF16), values) / total).astype(BF16)
+    def fixed(pair, count):
+        for c in pair:
+            begin, own_count = begin_of(c), count_of(c)
+            kat = pl.ds(pl.multiple_of(begin * BLK, BLK), count * BLK)
+            keys = xs[kat, 128:256]
+            values = xs[kat, 256:384]
+            mine = lax.broadcasted_iota(jnp.int32, (1, count * BLK), 1) < own_count * BLK
+            kp = jnp.where(mine, key_places(kat), 1e9)
+            for i in range(0, count, TILE):
+                wide = min(TILE, count - i)
+                at = pl.ds(pl.multiple_of((begin + i) * BLK, BLK), wide * BLK)
+                scores = hidden(nt_dot(xs[at, 0:128], keys), kp, dot(xs[at, 384:512], to_all))
+                weight = jnp.exp2(scores - jnp.max(scores, axis=1, keepdims=True))
+                total = jnp.sum(weight, axis=1, keepdims=True)
+                os[at, :] = (dot(weight.astype(BF16), values) / total).astype(BF16)
 
     def general(begin, count):
         def queries(i, _):
@@ -247,15 +277,23 @@
 
         lax.fori_loop(0, count, queries, 0)
 
-    def cluster(c, _):
-        begin = tab[0, 16 + c]
-        count = tab[0, 24 + c]
+    def clusters(k, _):
+        pair = [JOINT * k + u for u in range(JOINT)]
+        counts = [count_of(c) for c in pair]
+        most = functools.reduce(jnp.maximum, counts)
+        least = functools.reduce(jnp.minimum, counts)
+        alike = (most >= FIXED[0]) & (most <= FIXED[-1]) & (least >= most - 2)
         for n in FIXED:
-            pl.when(count == n)(functools.partial(fixed, begin, n))
-        pl.when((count < FIXED[0]) | (count > FIXED[-1]))(functools.partial(general, begin, count))
+            pl.when(alike & (most == n))(functools.partial(fixed, pair, n))
+
+        @pl.when(jnp.logical_not(alike))
+        def _():
+            for c, n in zip(pair, counts):
+                general(begin_of(c), n)
+
         return 0
 
-    lax.fori_loop(0, CL_SET, cluster, 0)
+    lax.fori_loop(0, CL_SET // JOINT, clusters, 0)
 
     code_lanes = iota((256, CODES), 1)
 
@@ -273,7 +311,9 @@
         else:
             o_ref[at] = (o_ref[at].astype(F32) + new).astype(BF16)
 
-    each_block(spread)
+    each_block(spread, after=lambda i: part_out(i).start())
+    for i in range(steps):
+        part_out(i).wait()
 
 
 def attend_call(slots, got):
@@ -282,21 +322,28 @@
     total_rows = sources * slots + (CL_SET + 4) * BLK
     return pl.pallas_call(
         functools.partial(attend_kernel, slots),
-        in_specs=[whole],
-        out_specs=[whole, whole],
+        in_specs=[pl.BlockSpec(memory_space=pl.ANY)],
+        out_specs=[pl.BlockSpec(memory_space=pl.ANY), whole],
         out_shape=[
             jax.ShapeDtypeStruct((sources, slots, 128), BF16),
             jax.ShapeDtypeStruct((8, 128), F32),
         ],
         scratch_shapes=[
+            pltpu.VMEM(got.shape, BF16),
+            pltpu.VMEM((sources, slots, 128), BF16),
+            pltpu.VMEM((sources, 16, 128), BF16),
+            pltpu.VMEM((sources * 8, 128), F32),
             pltpu.VMEM((total_rows, 4 * HEAD_DIM), BF16),
             pltpu.VMEM((total_rows, HEAD_DIM), BF16),
             pltpu.VMEM((sources, 128), F32),
             pltpu.VMEM((sources, 128), F32),
             pltpu.VMEM((sources, 128), F32),
-            pltpu.VMEM((sources, 128), jnp.int32),
-            pltpu.SMEM((sources, 128), jnp.int32),
+            pltpu.VMEM((sources + 16, 128), jnp.int32),
+            pltpu.SMEM((sources + 16, 128), jnp.int32),
             pltpu.SemaphoreType.DMA,
+            pltpu.SemaphoreType.DMA,
+            pltpu.SemaphoreType.DMA((sources // (4 * UNROLL),)),
+            pltpu.SemaphoreType.DMA((sources // (4 * UNROLL),)),
         ],
         compiler_params=pltpu.CompilerParams(vmem_limit_bytes=56 * 2**20),
         name="attend",

time: 149 us -> 147 us (0.987)
  Pallas kernels: 33.5 us -> 28.2 us
  starting transfers between devices: 7.2 us -> 11.1 us
    pallas_call x1, Pallas kernels: 26 us -> 20.7 us  [attend_call(): pl.pallas_call(functools.partial(attend_kernel, slots), in_specs=[pl.Bloc...]
    all_to_all x1, starting transfers between devices: 7.2 us -> 11.1 us  [attention(): lax.all_to_all(done, ('grp', 'blk'), split_axis=0, concat_axis=0, tiled=T...]
where the time goes in v4:
time: 147 us
  blocking collectives  79.8 us (54%)
  Pallas kernels  28.2 us (19%)
  waiting for transfers between devices  24.9 us (17%)
  starting transfers between devices  11.1 us (8%)
  local copies, waits for them, and re-layouts  2.2 us (1%)
    all_to_all x1, blocking collectives, attention(): lax.all_to_all(sent.reshape(sources, sent.shape[2], 128), ('grp', 'blk'),...  79.8 us
    all_to_all x1, waiting for transfers between devices, attention(): lax.all_to_all(done, ('grp', 'blk'), split_axis=0, concat_axis=0, tiled=T...  24.9 us
    pallas_call x1, Pallas kernels, attend_call(): pl.pallas_call(functools.partial(attend_kernel, slots), in_specs=[pl.Bloc...  20.7 us
    all_to_all x1, starting transfers between devices, attention(): lax.all_to_all(done, ('grp', 'blk'), split_axis=0, concat_axis=0, tiled=T...  11.1 us
    pallas_call x1, Pallas kernels, pack_call(): pl.pallas_call(functools.partial(pack_kernel, slots, sets), grid=(heads /...  5.75 us
  transfers between devices with their start and end apart: 1, of which 1 were waited for; matrix products, arithmetic and copies ran while one was open for 1% of the time, Pallas kernels for 0%

profile of v4, /device:TPU:0, one launch (start us, length us, event | category | flops | bytes accessed | tf_op | source)
XLA Modules:
  0.0 146.9 jit_solution(17302884487273495296)
XLA Ops:
  0.0 5.8 %pack.3 = (bf16[8,16,176,128]{3,2,1,0:T(8,128)(2,1)}, f32[1,256]{1,0:T(1,128)S(1)}) custom-call(s32[1,1]{1,0:T(1,128)} %bitcast.3.parity_ref, s32[1,256]{1,0:T(1,128)} %bitcast.12, s32[1,256]{1,0:T(1,128)} %bitcast.14, bf16[256,2048]{1,0:T(8,128)(2,1)} %q_ref.1, bf16[256,2048]{1,0:T(8,128)(2,1)} %k_ref.1, bf16[256,2048]{1,0:T(8,128)(2,1)} %v_ref.1), custom_call_target="tpu_custom_call" | custom-call | tf_op jit(solution)/shard_map/pack/pallas_call | solution.py:373
  5.8 79.8 %all_to_all.20.x_hbm = bf16[128,176,128]{2,1,0:T(8,128)(2,1)} all-to-all(bf16[128,176,128]{2,1,0:T(8,128)(2,1)} %bitcast.11), channel_id=1, replica_groups=mesh['grp'=16,'blk'=8] {'grp','blk'}, dimensions={0} | all-to-all | bytes 11534336 | tf_op jit(solution)/shard_map/all_to_all | solution.py:411
  85.6 0.0 copy-start
  85.6 0.0 copy-start.2
  85.6 0.0 copy-start.3
  85.6 20.7 %attend.3 = (bf16[128,56,128]{2,1,0:T(8,128)(2,1)}, f32[8,128]{1,0:T(8,128)}) custom-call(bf16[128,176,128]{2,1,0:T(8,128)(2,1)} %all_to_all.20.x_hbm), custom_call_target="tpu_custom_call" | custom-call | tf_op jit(solution)/shard_map/attend/pallas_call | solution.py:323
  106.4 11.1 %all-to-all-start.3 = ((bf16[128,56,128]{2,1,0:T(8,128)(2,1)}), bf16[128,56,128]{2,1,0:T(8,128)(2,1)S(1)}, u32[]{:S(2)}, u32[]{:S(2)}) async-start(bf16[128,56,128]{2,1,0:T(8,128)(2,1)} %get-tuple-element.42), calls=%async_computation.3 | async-start | bytes 3670016 | tf_op jit(solution)/shard_map/all_to_all | solution.py:415
  117.4 1.2 slice.3
  119.3 24.9 %all-to-all-done.3 = bf16[128,56,128]{2,1,0:T(8,128)(2,1)S(1)} async-done(((bf16[128,56,128]{2,1,0:T(8,128)(2,1)}), bf16[128,56,128]{2,1,0:T(8,128)(2,1)S(1)}, u32[]{:S(2)}, u32[]{:S(2)}) %all-to-all-start.3) | async-done | bytes 1835040 | tf_op jit(solution)/shard_map/all_to_all | solution.py:415
  144.2 0.0 copy-done
  144.2 0.0 copy-done.2
  144.2 0.0 copy-done.3
  144.2 1.8 %conditional.1 = (bf16[256,2048]{1,0:T(8,128)(2,1)S(1)}) conditional(s32[]{:T(128)} %bitcast.7, (bf16[128,56,128]{2,1,0:T(8,128)(2,1)S(1)}, f32[1,256]{1,0:T(1,128)S(1)}) %tuple.11, (s32[1,1]{1,0:T(1,128)}, s32[1,256]{1,0:T(1,128)S(1)}, s32[1,256]{1,0:T(1,128)S(1)}, bf16[256,2048]{1,0:T(8,128)(2,1)S(1)}, bf16[256,2048]{1,0:T(8,128)(2,1)}, ...), branch_computations={%region_0.1_spmd, %region_1.2_spmd} | conditional | bytes 17825800 | solution.py:419
  144.2 1.7 %unpack.2 = bf16[256,2048]{1,0:T(8,128)(2,1)S(1)} custom-call(f32[1,256]{1,0:T(1,128)S(1)} %get-tuple-element.25.slot_ref, bf16[8,16,56,128]{3,2,1,0:T(8,128)(2,1)S(1)} %bitcast.9), custom_call_target="tpu_custom_call" | custom-call | tf_op jit(solution)/shard_map/cond/branch_0_fun/unpack/pallas_call | solution.py:391
  146.0 0.0 copy-start.1
  146.0 1.0 copy-done.1
Async XLA Ops:
  85.6 58.6 %copy-start = (bf16[256,2048]{1,0:T(8,128)(2,1)S(1)}, bf16[256,2048]{1,0:T(8,128)(2,1)}, u32[]{:S(2)}) copy-start(bf16[256,2048]{1,0:T(8,128)(2,1)} %q_ref.1) | copy-start | bytes 3145732
  85.6 58.6 %copy-start.2 = (s32[256]{0:T(256)S(1)}, s32[256]{0:T(256)}, u32[]{:S(2)}) copy-start(s32[256]{0:T(256)} %param.10) | copy-start | bytes 3076
  85.6 58.6 %copy-start.3 = (s32[256]{0:T(256)S(1)}, s32[256]{0:T(256)}, u32[]{:S(2)}) copy-start(s32[256]{0:T(256)} %param.11) | copy-start | bytes 3076
  106.4 37.8 %all-to-all-start.3 = ((bf16[128,56,128]{2,1,0:T(8,128)(2,1)}), bf16[128,56,128]{2,1,0:T(8,128)(2,1)S(1)}, u32[]{:S(2)}, u32[]{:S(2)}) async-start(bf16[128,56,128]{2,1,0:T(8,128)(2,1)} %get-tuple-element.42), calls=%async_computation.3 | async-start | bytes 3670016 | tf_op jit(solution)/shard_map/all_to_all | solution.py:415
  146.0 1.0 copy-start.1

commit v5 on v4

--- a/solution.py
+++ b/solution.py
@@ -14,7 +14,7 @@
 CODES = CL_SET * RUN
 BLK = 128
 FIXED = (4, 5, 6)
-UNROLL = 8
+UNROLL = 16
 TILE = 3
 JOINT = 2
 ALL = 64
@@ -80,16 +80,17 @@
         meta[4:5, :] = jnp.broadcast_to(short, (1, sets * 128))
 
     gap = out_ref.shape[2] - 3 * slots - 8
-    for h in range(out_ref.shape[1]):
-        at = slice(h * HEAD_DIM, (h + 1) * HEAD_DIM)
+    for h in range(0, out_ref.shape[1], 2):
+        at = slice(h * HEAD_DIM, (h + 2) * HEAD_DIM)
         y = dot(place[...], jnp.concatenate([q_ref[:, at], k_ref[:, at], v_ref[:, at]], axis=1))
         for s in range(sets):
             part = y[s * slots : (s + 1) * slots]
-            pieces = [part[:, :128], part[:, 128:256], part[:, 256:]]
-            if gap:
-                pieces.append(jnp.zeros((gap, 128), F32))
-            pieces.append(meta[0:8, s * 128 : (s + 1) * 128])
-            out_ref[s, h] = jnp.concatenate(pieces, axis=0).astype(BF16)
+            for u in range(2):
+                pieces = [part[:, i * 128 : (i + 1) * 128] for i in (u, u + 2, u + 4)]
+                if gap:
+                    pieces.append(jnp.zeros((gap, 128), F32))
+                pieces.append(meta[0:8, s * 128 : (s + 1) * 128])
+                out_ref[s, h + u] = jnp.concatenate(pieces, axis=0).astype(BF16)
 
 
 def attend_kernel(
@@ -98,6 +99,7 @@
     sources, rows, _ = x_ref.shape
     step_rows = 4 * UNROLL
     steps = sources // step_rows
+    blocks = sources // 4
     facts_in = pltpu.make_async_copy(x_hbm.at[:, rows - 16 : rows, :], facts_ref, facts_sem)
     facts_in.start()
 
@@ -148,21 +150,26 @@
         place = place + is_own[c] * shift[:, c * 128 : (c + 1) * 128]
     step = jnp.floor(place * (1.0 / RUN) + (0.5 / RUN))
     code[...] = jnp.where(own > 0.0, step * CODES + (own - 1.0) * RUN + (place - step * RUN) + 1.0, 0.0)
-    passes = jnp.max(jnp.where(lane < CL_SET, after_block - skipped, 0.0), axis=(0, 1), keepdims=True)
-    passes = jnp.floor((passes + (RUN - 1)) * (1.0 / RUN))
-    tab_v[0:sources] = jnp.where(lane < CL_SET, start_blk * BLK + skipped, passes).astype(jnp.int32)
-    tab_v[sources : sources + 8] = start_blk[0:8].astype(jnp.int32)
-    tab_v[sources + 8 : sources + 16] = nblk[0:8].astype(jnp.int32)
+    passes = jnp.where(lane < CL_SET, jnp.floor((after_block - skipped + (RUN - 1)) * (1.0 / RUN)), 0.0)
+    most = jnp.max(passes, axis=(0, 1), keepdims=True)
+    table = jnp.where(lane < 2 * CL_SET, pltpu.roll(passes, CL_SET, 1), most)
+    flat[0:sources] = jnp.where(lane < CL_SET, start_blk * BLK + skipped, table)
+    tab_v[0:blocks] = flat[pl.ds(0, blocks, 4), :].astype(jnp.int32)
+    tab_v[blocks : blocks + 8] = start_blk[0:8].astype(jnp.int32)
+    tab_v[blocks + 8 :] = nblk[0:8].astype(jnp.int32)
     copy = pltpu.make_async_copy(tab_v, tab, sem)
     copy.start()
     copy.wait()
-    most_passes = tab[0, CL_SET]
+    most_passes = tab[0, 2 * CL_SET]
 
     def begin_of(c):
-        return tab[sources, c]
+        return tab[blocks, c]
 
     def count_of(c):
-        return tab[sources + 8, c]
+        return tab[blocks + 8, c]
+
+    def passes_of(b):
+        return functools.reduce(jnp.maximum, [tab[b, CL_SET + c] for c in range(CL_SET)])
 
     used_blocks = begin_of(CL_SET - 1) + count_of(CL_SET - 1)
 
@@ -189,10 +196,11 @@
         x4 = x_ref[pl.ds(4 * b, 4)].astype(F32)
         xcat = jnp.concatenate([x4[:, i * slots : i * slots + 64].reshape(256, 128) for i in range(3)], axis=1).astype(BF16)
         row = joined(code, b) - jnp.asarray(p * CODES + 1, F32)
-        where_at = jnp.where(which == 0, joined(high, b), jnp.where(which == 1, joined(low, b), 0.0)).astype(BF16)
+        where_at = jnp.where(which == 0, joined(high, b), jnp.where(which == 1, joined(low, b), 0.0))
+        xcat = jnp.concatenate([xcat, jnp.transpose(where_at).astype(BF16)], axis=1)
         select = jnp.where(code_rows == row, 1.0, 0.0).astype(BF16)
-        y = jnp.concatenate([dot(select, xcat), nt_dot(select, where_at)], axis=1).astype(BF16)
-        ats = [pl.ds(pl.multiple_of(tab[4 * b, c] + p * RUN, 16), RUN) for c in range(CL_SET)]
+        y = dot(select, xcat).astype(BF16)
+        ats = [pl.ds(pl.multiple_of(tab[b, c] + p * RUN, 16), RUN) for c in range(CL_SET)]
         new = [xs[at, :] + y[c * RUN : (c + 1) * RUN] for c, at in enumerate(ats)]
         for at, x in zip(ats, new):
             xs[at, :] = x
@@ -213,7 +221,7 @@
                         body(b, p)
                         return 0
 
-                    return lax.fori_loop(1, most_passes, more, 0)
+                    return lax.fori_loop(1, passes_of(b), more, 0)
 
                 lax.fori_loop(0, UNROLL, rest, 0)
 
@@ -301,7 +309,7 @@
         col = column(joined(code, b) - jnp.asarray(p * CODES + 1, F32))
         col = jnp.concatenate([col] * (CODES // 128), axis=1)
         cat = jnp.concatenate(
-            [os[pl.ds(pl.multiple_of(tab[4 * b, c] + p * RUN, 16), RUN), :] for c in range(CL_SET)], axis=0
+            [os[pl.ds(pl.multiple_of(tab[b, c] + p * RUN, 16), RUN), :] for c in range(CL_SET)], axis=0
         )
         select = jnp.where(code_lanes == col, 1.0, 0.0).astype(BF16)
         new = dot(select, cat).reshape(4, 64, 128)[:, :slots]
@@ -338,8 +346,8 @@
             pltpu.VMEM((sources, 128), F32),
             pltpu.VMEM((sources, 128), F32),
             pltpu.VMEM((sources, 128), F32),
-            pltpu.VMEM((sources + 16, 128), jnp.int32),
-            pltpu.SMEM((sources + 16, 128), jnp.int32),
+            pltpu.VMEM((sources // 4 + 16, 128), jnp.int32),
+            pltpu.SMEM((sources // 4 + 16, 128), jnp.int32),
             pltpu.SemaphoreType.DMA,
             pltpu.SemaphoreType.DMA,
             pltpu.SemaphoreType.DMA((sources // (4 * UNROLL),)),

time: 147 us -> 143 us (0.973)
  starting transfers between devices: 11.1 us -> 6.02 us
    all_to_all x1, starting transfers between devices: 11.1 us -> 6.02 us  [attention(): lax.all_to_all(done, ('grp', 'blk'), split_axis=0, concat_axis=0, tiled=T...]
where the time goes in v5:
time: 143 us; the launch traced here: 142 us
  blocking collectives  79.8 us (56%)
  Pallas kernels  28.6 us (20%)
  waiting for transfers between devices  24.9 us (17%)
  starting transfers between devices  6.02 us (4%)
  local copies, waits for them, and re-layouts  2.2 us (2%)
    all_to_all x1, blocking collectives, attention(): lax.all_to_all(sent.reshape(sources, sent.shape[2], 128), ('grp', 'blk'),...  79.8 us
    all_to_all x1, waiting for transfers between devices, attention(): lax.all_to_all(done, ('grp', 'blk'), split_axis=0, concat_axis=0, tiled=T...  24.9 us
    pallas_call x1, Pallas kernels, attend_call(): pl.pallas_call(functools.partial(attend_kernel, slots), in_specs=[pl.Bloc...  21.7 us
    all_to_all x1, starting transfers between devices, attention(): lax.all_to_all(done, ('grp', 'blk'), split_axis=0, concat_axis=0, tiled=T...  6.02 us
    pallas_call x1, Pallas kernels, pack_call(): pl.pallas_call(functools.partial(pack_kernel, slots, sets), grid=(heads /...  5.23 us
  transfers between devices with their start and end apart: 1, of which 1 were waited for; matrix products, arithmetic and copies ran while one was open for 1% of the time, Pallas kernels for 0%

profile of v5, /device:TPU:0, one launch (start us, length us, event | category | flops | bytes accessed | tf_op | source)
XLA Modules:
  0.0 142.3 jit_solution(2378939504644652567)
XLA Ops:
  0.0 5.2 %pack.3 = (bf16[8,16,176,128]{3,2,1,0:T(8,128)(2,1)}, f32[1,256]{1,0:T(1,128)S(1)}) custom-call(s32[1,1]{1,0:T(1,128)} %bitcast.3.parity_ref, s32[1,256]{1,0:T(1,128)} %bitcast.12, s32[1,256]{1,0:T(1,128)} %bitcast.14, bf16[256,2048]{1,0:T(8,128)(2,1)} %q_ref.1, bf16[256,2048]{1,0:T(8,128)(2,1)} %k_ref.1, bf16[256,2048]{1,0:T(8,128)(2,1)} %v_ref.1), custom_call_target="tpu_custom_call" | custom-call | tf_op jit(solution)/shard_map/pack/pallas_call | solution.py:381
  5.2 79.8 %all_to_all.20.x_hbm = bf16[128,176,128]{2,1,0:T(8,128)(2,1)} all-to-all(bf16[128,176,128]{2,1,0:T(8,128)(2,1)} %bitcast.11), channel_id=1, replica_groups=mesh['grp'=16,'blk'=8] {'grp','blk'}, dimensions={0} | all-to-all | bytes 11534336 | tf_op jit(solution)/shard_map/all_to_all | solution.py:419
  85.1 0.0 copy-start
  85.1 0.0 copy-start.2
  85.1 0.0 copy-start.3
  85.1 21.7 %attend.3 = (bf16[128,56,128]{2,1,0:T(8,128)(2,1)}, f32[8,128]{1,0:T(8,128)}) custom-call(bf16[128,176,128]{2,1,0:T(8,128)(2,1)} %all_to_all.20.x_hbm), custom_call_target="tpu_custom_call" | custom-call | tf_op jit(solution)/shard_map/attend/pallas_call | solution.py:331
  106.8 6.0 %all-to-all-start.3 = ((bf16[128,56,128]{2,1,0:T(8,128)(2,1)}), bf16[128,56,128]{2,1,0:T(8,128)(2,1)S(1)}, u32[]{:S(2)}, u32[]{:S(2)}) async-start(bf16[128,56,128]{2,1,0:T(8,128)(2,1)} %get-tuple-element.42), calls=%async_computation.3 | async-start | bytes 3670016 | tf_op jit(solution)/shard_map/all_to_all | solution.py:423
  112.8 1.2 slice.3
  114.7 24.9 %all-to-all-done.3 = bf16[128,56,128]{2,1,0:T(8,128)(2,1)S(1)} async-done(((bf16[128,56,128]{2,1,0:T(8,128)(2,1)}), bf16[128,56,128]{2,1,0:T(8,128)(2,1)S(1)}, u32[]{:S(2)}, u32[]{:S(2)}) %all-to-all-start.3) | async-done | bytes 1835040 | tf_op jit(solution)/shard_map/all_to_all | solution.py:423
  139.6 0.0 copy-done
  139.6 0.0 copy-done.2
  139.6 0.0 copy-done.3
  139.6 1.8 %conditional.1 = (bf16[256,2048]{1,0:T(8,128)(2,1)S(1)}) conditional(s32[]{:T(128)} %bitcast.7, (bf16[128,56,128]{2,1,0:T(8,128)(2,1)S(1)}, f32[1,256]{1,0:T(1,128)S(1)}) %tuple.11, (s32[1,1]{1,0:T(1,128)}, s32[1,256]{1,0:T(1,128)S(1)}, s32[1,256]{1,0:T(1,128)S(1)}, bf16[256,2048]{1,0:T(8,128)(2,1)S(1)}, bf16[256,2048]{1,0:T(8,128)(2,1)}, ...), branch_computations={%region_0.1_spmd, %region_1.2_spmd} | conditional | bytes 17825800 | solution.py:427
  139.6 1.7 %unpack.2 = bf16[256,2048]{1,0:T(8,128)(2,1)S(1)} custom-call(f32[1,256]{1,0:T(1,128)S(1)} %get-tuple-element.25.slot_ref, bf16[8,16,56,128]{3,2,1,0:T(8,128)(2,1)S(1)} %bitcast.9), custom_call_target="tpu_custom_call" | custom-call | tf_op jit(solution)/shard_map/cond/branch_0_fun/unpack/pallas_call | solution.py:399
  141.3 0.0 copy-start.1
  141.3 1.0 copy-done.1
Async XLA Ops:
  85.1 54.5 %copy-start = (bf16[256,2048]{1,0:T(8,128)(2,1)S(1)}, bf16[256,2048]{1,0:T(8,128)(2,1)}, u32[]{:S(2)}) copy-start(bf16[256,2048]{1,0:T(8,128)(2,1)} %q_ref.1) | copy-start | bytes 3145732
  85.1 54.5 %copy-start.2 = (s32[256]{0:T(256)S(1)}, s32[256]{0:T(256)}, u32[]{:S(2)}) copy-start(s32[256]{0:T(256)} %param.10) | copy-start | bytes 3076
  85.1 54.5 %copy-start.3 = (s32[256]{0:T(256)S(1)}, s32[256]{0:T(256)}, u32[]{:S(2)}) copy-start(s32[256]{0:T(256)} %param.11) | copy-start | bytes 3076
  106.8 32.8 %all-to-all-start.3 = ((bf16[128,56,128]{2,1,0:T(8,128)(2,1)}), bf16[128,56,128]{2,1,0:T(8,128)(2,1)S(1)}, u32[]{:S(2)}, u32[]{:S(2)}) async-start(bf16[128,56,128]{2,1,0:T(8,128)(2,1)} %get-tuple-element.42), calls=%async_computation.3 | async-start | bytes 3670016 | tf_op jit(solution)/shard_map/all_to_all | solution.py:423
  141.3 1.0 copy-start.1

commit v6 on v5

--- a/solution.py
+++ b/solution.py
@@ -353,7 +353,7 @@
             pltpu.SemaphoreType.DMA((sources // (4 * UNROLL),)),
             pltpu.SemaphoreType.DMA((sources // (4 * UNROLL),)),
         ],
-        compiler_params=pltpu.CompilerParams(vmem_limit_bytes=56 * 2**20),
+        compiler_params=pltpu.CompilerParams(vmem_limit_bytes=32 * 2**20),
         name="attend",
     )(got)
 
@@ -388,7 +388,7 @@
             jax.ShapeDtypeStruct((1, tokens), F32),
         ],
         scratch_shapes=[pltpu.VMEM((sets * slots, tokens), BF16), pltpu.VMEM((16, sets * 128), F32)],
-        compiler_params=pltpu.CompilerParams(vmem_limit_bytes=56 * 2**20),
+        compiler_params=pltpu.CompilerParams(vmem_limit_bytes=20 * 2**20),
         name="pack",
     )(parity, cid_row, pos_row, queries, keys, values)
 
@@ -406,7 +406,7 @@
         out_specs=pl.BlockSpec((tokens, UNPACK * HEAD_DIM), lambda h: (0, h)),
         out_shape=jax.ShapeDtypeStruct((tokens, heads * HEAD_DIM), BF16),
         scratch_shapes=[pltpu.VMEM((tokens, sets * slots), BF16)],
-        compiler_params=pltpu.CompilerParams(vmem_limit_bytes=56 * 2**20),
+        compiler_params=pltpu.CompilerParams(vmem_limit_bytes=16 * 2**20),
         name="unpack",
     )(slot, back)
 

time: 143 us -> 138 us (0.965); the launches traced: 142 us -> 139 us
  Pallas kernels: 28.6 us -> 23.9 us
  starting transfers between devices: 6.02 us -> 7.71 us
    pallas_call x1, Pallas kernels: 21.7 us -> 18.1 us  [attend_call(): pl.pallas_call(functools.partial(attend_kernel, slots), in_specs=[pl.Bloc...]
    all_to_all x1, starting transfers between devices: 6.02 us -> 7.71 us  [attention(): lax.all_to_all(done, ('grp', 'blk'), split_axis=0, concat_axis=0, tiled=T...]
  transfers between devices with their start and end apart: 1 -> 1, of which waited for: 1 -> 1; matrix products, arithmetic and copies ran while one was open for 1% -> 0% of each run, Pallas kernels for 0% -> 0%
where the time goes in v6:
time: 138 us; the launch traced here: 139 us
  blocking collectives  79.5 us (58%)
  waiting for transfers between devices  25.6 us (19%)
  Pallas kernels  23.9 us (17%)
  starting transfers between devices  7.71 us (6%)
  local copies, waits for them, and re-layouts  1.49 us (1%)
    all_to_all x1, blocking collectives, attention(): lax.all_to_all(sent.reshape(sources, sent.shape[2], 128), ('grp', 'blk'),...  79.5 us
    all_to_all x1, waiting for transfers between devices, attention(): lax.all_to_all(done, ('grp', 'blk'), split_axis=0, concat_axis=0, tiled=T...  25.6 us
    pallas_call x1, Pallas kernels, attend_call(): pl.pallas_call(functools.partial(attend_kernel, slots), in_specs=[pl.Bloc...  18.1 us
    all_to_all x1, starting transfers between devices, attention(): lax.all_to_all(done, ('grp', 'blk'), split_axis=0, concat_axis=0, tiled=T...  7.71 us
    pallas_call x1, Pallas kernels, pack_call(): pl.pallas_call(functools.partial(pack_kernel, slots, sets), grid=(heads /...  3.96 us
  transfers between devices with their start and end apart: 1, of which 1 were waited for; matrix products, arithmetic and copies ran while one was open for 0% of the time, Pallas kernels for 0%

profile of v6, /device:TPU:0, one launch (start us, length us, event | category | flops | bytes accessed | tf_op | source)
XLA Modules:
  0.0 138.9 jit_solution(10949686287741885321)
XLA Ops:
  0.0 4.0 %pack.3 = (bf16[8,16,176,128]{3,2,1,0:T(8,128)(2,1)S(1)}, f32[1,256]{1,0:T(1,128)S(1)}) custom-call(s32[1,1]{1,0:T(1,128)} %bitcast.3.parity_ref, s32[1,256]{1,0:T(1,128)} %bitcast.12, s32[1,256]{1,0:T(1,128)} %bitcast.14, bf16[256,2048]{1,0:T(8,128)(2,1)} %q_ref.1, bf16[256,2048]{1,0:T(8,128)(2,1)} %k_ref.1, bf16[256,2048]{1,0:T(8,128)(2,1)} %v_ref.1), custom_call_target="tpu_custom_call" | custom-call | tf_op jit(solution)/shard_map/pack/pallas_call | solution.py:381
  4.0 79.5 %all_to_all.20.x_hbm = bf16[128,176,128]{2,1,0:T(8,128)(2,1)S(1)} all-to-all(bf16[128,176,128]{2,1,0:T(8,128)(2,1)S(1)} %bitcast.10), channel_id=1, replica_groups=mesh['grp'=16,'blk'=8] {'grp','blk'}, dimensions={0} | all-to-all | bytes 11534336 | tf_op jit(solution)/shard_map/all_to_all | solution.py:419
  83.5 0.0 copy-start
  83.5 0.0 copy-start.2
  83.5 0.0 copy-start.3
  83.5 18.1 %attend.3 = (bf16[128,56,128]{2,1,0:T(8,128)(2,1)}, f32[8,128]{1,0:T(8,128)S(1)}) custom-call(bf16[128,176,128]{2,1,0:T(8,128)(2,1)S(1)} %all_to_all.20.x_hbm), custom_call_target="tpu_custom_call" | custom-call | tf_op jit(solution)/shard_map/attend/pallas_call | solution.py:331
  101.7 7.7 %all-to-all-start.3 = ((bf16[128,56,128]{2,1,0:T(8,128)(2,1)}), bf16[128,56,128]{2,1,0:T(8,128)(2,1)S(1)}, u32[]{:S(2)}, u32[]{:S(2)}) async-start(bf16[128,56,128]{2,1,0:T(8,128)(2,1)} %get-tuple-element.42), calls=%async_computation.3 | async-start | bytes 3670016 | tf_op jit(solution)/shard_map/all_to_all | solution.py:423
  109.4 0.5 slice.3
  110.6 25.6 %all-to-all-done.3 = bf16[128,56,128]{2,1,0:T(8,128)(2,1)S(1)} async-done(((bf16[128,56,128]{2,1,0:T(8,128)(2,1)}), bf16[128,56,128]{2,1,0:T(8,128)(2,1)S(1)}, u32[]{:S(2)}, u32[]{:S(2)}) %all-to-all-start.3) | async-done | bytes 1835040 | tf_op jit(solution)/shard_map/all_to_all | solution.py:423
  136.2 0.0 copy-done
  136.2 0.0 copy-done.2
  136.2 0.0 copy-done.3
  136.2 1.8 %conditional.1 = (bf16[256,2048]{1,0:T(8,128)(2,1)S(1)}) conditional(s32[]{:T(128)} %bitcast.7, (bf16[128,56,128]{2,1,0:T(8,128)(2,1)S(1)}, f32[1,256]{1,0:T(1,128)S(1)}) %tuple.11, (s32[1,1]{1,0:T(1,128)}, s32[1,256]{1,0:T(1,128)S(1)}, s32[1,256]{1,0:T(1,128)S(1)}, bf16[256,2048]{1,0:T(8,128)(2,1)S(1)}, bf16[256,2048]{1,0:T(8,128)(2,1)}, ...), branch_computations={%region_0.1_spmd, %region_1.2_spmd} | conditional | bytes 17825800 | solution.py:427
  136.2 1.7 %unpack.2 = bf16[256,2048]{1,0:T(8,128)(2,1)S(1)} custom-call(f32[1,256]{1,0:T(1,128)S(1)} %get-tuple-element.25.slot_ref, bf16[8,16,56,128]{3,2,1,0:T(8,128)(2,1)S(1)} %bitcast.11), custom_call_target="tpu_custom_call" | custom-call | tf_op jit(solution)/shard_map/cond/branch_0_fun/unpack/pallas_call | solution.py:399
  137.9 0.0 copy-start.1
  138.0 1.0 copy-done.1
Async XLA Ops:
  83.5 52.6 %copy-start = (bf16[256,2048]{1,0:T(8,128)(2,1)S(1)}, bf16[256,2048]{1,0:T(8,128)(2,1)}, u32[]{:S(2)}) copy-start(bf16[256,2048]{1,0:T(8,128)(2,1)} %q_ref.1) | copy-start | bytes 3145732
  83.5 52.6 %copy-start.2 = (s32[256]{0:T(256)S(1)}, s32[256]{0:T(256)}, u32[]{:S(2)}) copy-start(s32[256]{0:T(256)} %param.10) | copy-start | bytes 3076
  83.5 52.6 %copy-start.3 = (s32[256]{0:T(256)S(1)}, s32[256]{0:T(256)}, u32[]{:S(2)}) copy-start(s32[256]{0:T(256)} %param.11) | copy-start | bytes 3076
  101.7 34.5 %all-to-all-start.3 = ((bf16[128,56,128]{2,1,0:T(8,128)(2,1)}), bf16[128,56,128]{2,1,0:T(8,128)(2,1)S(1)}, u32[]{:S(2)}, u32[]{:S(2)}) async-start(bf16[128,56,128]{2,1,0:T(8,128)(2,1)} %get-tuple-element.42), calls=%async_computation.3 | async-start | bytes 3670016 | tf_op jit(solution)/shard_map/all_to_all | solution.py:423
  137.9 1.0 copy-start.1

commit v7 on v6

--- a/solution.py
+++ b/solution.py
@@ -93,33 +93,14 @@
                 out_ref[s, h + u] = jnp.concatenate(pieces, axis=0).astype(BF16)
 
 
-def attend_kernel(
-    slots, x_hbm, o_hbm, short_ref, x_ref, o_ref, facts_ref, flat, xs, os, code, high, low, tab_v, tab, sem, facts_sem, in_sems, out_sems
-):
+def attend_kernel(slots, x_ref, o_ref, short_ref, flat, xs, os, code, high, low, tab_v, tab, sem):
     sources, rows, _ = x_ref.shape
-    step_rows = 4 * UNROLL
-    steps = sources // step_rows
     blocks = sources // 4
-    facts_in = pltpu.make_async_copy(x_hbm.at[:, rows - 16 : rows, :], facts_ref, facts_sem)
-    facts_in.start()
-
-    def part_in(i):
-        at = pl.ds(i * step_rows, step_rows)
-        return pltpu.make_async_copy(x_hbm.at[at], x_ref.at[at], in_sems.at[i])
-
-    def part_out(i):
-        at = pl.ds(i * step_rows, step_rows)
-        return pltpu.make_async_copy(o_ref.at[at], o_hbm.at[at], out_sems.at[i])
-
-    for i in range(steps):
-        part_in(i).start()
+    total_rows = xs.shape[0]
     os[...] = jnp.zeros(os.shape, BF16)
     ahead = 5 * sources // 16
     xs[0 : ahead * BLK, :] = jnp.zeros((ahead * BLK, xs.shape[1]), BF16)
-    facts_in.wait()
-    total_rows = xs.shape[0]
-
-    flat[...] = facts_ref[...].astype(F32)[:, 8:16].reshape(flat.shape)
+    flat[...] = x_ref[:, rows - 16 : rows, :].astype(F32)[:, 8:16].reshape(flat.shape)
 
     def fact(i):
         return flat[pl.ds(i, sources, 8), :]
@@ -205,10 +186,8 @@
         for at, x in zip(ats, new):
             xs[at, :] = x
 
-    def each_block(body, before=None, after=None):
+    def each_block(body):
         def some(i, _):
-            if before is not None:
-                before(i)
             for u in range(UNROLL):
                 body(i * UNROLL + u, 0)
 
@@ -225,13 +204,11 @@
 
                 lax.fori_loop(0, UNROLL, rest, 0)
 
-            if after is not None:
-                after(i)
             return 0
 
-        lax.fori_loop(0, steps, some, 0)
-
-    each_block(compact, before=lambda i: part_in(i).wait())
+        lax.fori_loop(0, blocks // UNROLL, some, 0)
+
+    each_block(compact)
 
     scale = HEAD_DIM ** (-0.5) * 1.4426950408889634
     to_lanes = jnp.where(lax.broadcasted_iota(jnp.int32, (16, 128), 1) < 2, 1.0, 0.0).astype(BF16)
@@ -319,9 +296,7 @@
         else:
             o_ref[at] = (o_ref[at].astype(F32) + new).astype(BF16)
 
-    each_block(spread, after=lambda i: part_out(i).start())
-    for i in range(steps):
-        part_out(i).wait()
+    each_block(spread)
 
 
 def attend_call(slots, got):
@@ -330,16 +305,13 @@
     total_rows = sources * slots + (CL_SET + 4) * BLK
     return pl.pallas_call(
         functools.partial(attend_kernel, slots),
-        in_specs=[pl.BlockSpec(memory_space=pl.ANY)],
-        out_specs=[pl.BlockSpec(memory_space=pl.ANY), whole],
+        in_specs=[whole],
+        out_specs=[whole, whole],
         out_shape=[
-            jax.ShapeDtypeStruct((sources, slots, 128), BF16),
+            pltpu.VMEM((sources, slots, 128), BF16),
             jax.ShapeDtypeStruct((8, 128), F32),
         ],
         scratch_shapes=[
-            pltpu.VMEM(got.shape, BF16),
-            pltpu.VMEM((sources, slots, 128), BF16),
-            pltpu.VMEM((sources, 16, 128), BF16),
             pltpu.VMEM((sources * 8, 128), F32),
             pltpu.VMEM((total_rows, 4 * HEAD_DIM), BF16),
             pltpu.VMEM((total_rows, HEAD_DIM), BF16),
@@ -349,13 +321,10 @@
             pltpu.VMEM((sources // 4 + 16, 128), jnp.int32),
             pltpu.SMEM((sources // 4 + 16, 128), jnp.int32),
             pltpu.SemaphoreType.DMA,
-            pltpu.SemaphoreType.DMA,
-            pltpu.SemaphoreType.DMA((sources // (4 * UNROLL),)),
-            pltpu.SemaphoreType.DMA((sources // (4 * UNROLL),)),
         ],
         compiler_params=pltpu.CompilerParams(vmem_limit_bytes=32 * 2**20),
         name="attend",
-    )(got)
+    )(pltpu.with_memory_space_constraint(got, pltpu.VMEM))
 
 
 def unpack_kernel(slots, slot_ref, r_ref, out_ref, select):

time: 138 us -> 140 us (1.014); the launches traced: 139 us -> 139 us
  starting transfers between devices: 7.71 us -> 5.04 us
  Pallas kernels: 23.9 us -> 26.4 us
    all_to_all x1, starting transfers between devices: 7.71 us -> 5.04 us  [attention(): lax.all_to_all(done, ('grp', 'blk'), split_axis=0, concat_axis=0, tiled=T...]
    pallas_call x1, Pallas kernels: 18.1 us -> 20.7 us  [attend_call(): pl.pallas_call(functools.partial(attend_kernel, slots), in_specs=[whole],...]
where the time goes in v7:
time: 140 us; the launch traced here: 139 us
  blocking collectives  79.5 us (57%)
  Pallas kernels  26.4 us (19%)
  waiting for transfers between devices  25.6 us (18%)
  starting transfers between devices  5.04 us (4%)
  local copies, waits for them, and re-layouts  1.49 us (1%)
    all_to_all x1, blocking collectives, attention(): lax.all_to_all(sent.reshape(sources, sent.shape[2], 128), ('grp', 'blk'),...  79.5 us
    all_to_all x1, waiting for transfers between devices, attention(): lax.all_to_all(done, ('grp', 'blk'), split_axis=0, concat_axis=0, tiled=T...  25.6 us
    pallas_call x1, Pallas kernels, attend_call(): pl.pallas_call(functools.partial(attend_kernel, slots), in_specs=[whole],...  20.7 us
    all_to_all x1, starting transfers between devices, attention(): lax.all_to_all(done, ('grp', 'blk'), split_axis=0, concat_axis=0, tiled=T...  5.04 us
    pallas_call x1, Pallas kernels, pack_call(): pl.pallas_call(functools.partial(pack_kernel, slots, sets), grid=(heads /...  3.96 us
  transfers between devices with their start and end apart: 1, of which 1 were waited for; matrix products, arithmetic and copies ran while one was open for 0% of the time, Pallas kernels for 0%

profile of v7, /device:TPU:0, one launch (start us, length us, event | category | flops | bytes accessed | tf_op | source)
XLA Modules:
  0.0 138.7 jit_solution(16637895272818061031)
XLA Ops:
  0.0 4.0 %pack.3 = (bf16[8,16,176,128]{3,2,1,0:T(8,128)(2,1)S(1)}, f32[1,256]{1,0:T(1,128)S(1)}) custom-call(s32[1,1]{1,0:T(1,128)} %bitcast.3.parity_ref, s32[1,256]{1,0:T(1,128)} %bitcast.12, s32[1,256]{1,0:T(1,128)} %bitcast.14, bf16[256,2048]{1,0:T(8,128)(2,1)} %q_ref.1, bf16[256,2048]{1,0:T(8,128)(2,1)} %k_ref.1, bf16[256,2048]{1,0:T(8,128)(2,1)} %v_ref.1), custom_call_target="tpu_custom_call" | custom-call | tf_op jit(solution)/shard_map/pack/pallas_call | solution.py:350
  4.0 79.5 %all_to_all.20.x_ref = bf16[128,176,128]{2,1,0:T(8,128)(2,1)S(1)} all-to-all(bf16[128,176,128]{2,1,0:T(8,128)(2,1)S(1)} %bitcast.10), channel_id=1, replica_groups=mesh['grp'=16,'blk'=8] {'grp','blk'}, dimensions={0} | all-to-all | bytes 11534336 | tf_op jit(solution)/shard_map/all_to_all | solution.py:388
  83.5 0.0 copy-start
  83.5 0.0 copy-start.2
  83.5 0.0 copy-start.3
  83.5 20.7 %attend.3 = (bf16[128,56,128]{2,1,0:T(8,128)(2,1)}, f32[8,128]{1,0:T(8,128)S(1)}) custom-call(bf16[128,176,128]{2,1,0:T(8,128)(2,1)S(1)} %all_to_all.20.x_ref), custom_call_target="tpu_custom_call" | custom-call | tf_op jit(solution)/shard_map/attend/pallas_call | solution.py:306
  104.2 5.0 %all-to-all-start.3 = ((bf16[128,56,128]{2,1,0:T(8,128)(2,1)}), bf16[128,56,128]{2,1,0:T(8,128)(2,1)S(1)}, u32[]{:S(2)}, u32[]{:S(2)}) async-start(bf16[128,56,128]{2,1,0:T(8,128)(2,1)} %get-tuple-element.42), calls=%async_computation.3 | async-start | bytes 3670016 | tf_op jit(solution)/shard_map/all_to_all | solution.py:392
  109.2 0.5 slice.3
  110.4 25.6 %all-to-all-done.3 = bf16[128,56,128]{2,1,0:T(8,128)(2,1)S(1)} async-done(((bf16[128,56,128]{2,1,0:T(8,128)(2,1)}), bf16[128,56,128]{2,1,0:T(8,128)(2,1)S(1)}, u32[]{:S(2)}, u32[]{:S(2)}) %all-to-all-start.3) | async-done | bytes 1835040 | tf_op jit(solution)/shard_map/all_to_all | solution.py:392
  136.0 0.0 copy-done
  136.0 0.0 copy-done.2
  136.0 0.0 copy-done.3
  136.0 1.8 %conditional.1 = (bf16[256,2048]{1,0:T(8,128)(2,1)S(1)}) conditional(s32[]{:T(128)} %bitcast.7, (bf16[128,56,128]{2,1,0:T(8,128)(2,1)S(1)}, f32[1,256]{1,0:T(1,128)S(1)}) %tuple.11, (s32[1,1]{1,0:T(1,128)}, s32[1,256]{1,0:T(1,128)S(1)}, s32[1,256]{1,0:T(1,128)S(1)}, bf16[256,2048]{1,0:T(8,128)(2,1)S(1)}, bf16[256,2048]{1,0:T(8,128)(2,1)}, ...), branch_computations={%region_0.1_spmd, %region_1.2_spmd} | conditional | bytes 17825800 | solution.py:396
  136.0 1.7 %unpack.2 = bf16[256,2048]{1,0:T(8,128)(2,1)S(1)} custom-call(f32[1,256]{1,0:T(1,128)S(1)} %get-tuple-element.25.slot_ref, bf16[8,16,56,128]{3,2,1,0:T(8,128)(2,1)S(1)} %bitcast.11), custom_call_target="tpu_custom_call" | custom-call | tf_op jit(solution)/shard_map/cond/branch_0_fun/unpack/pallas_call | solution.py:368
  137.8 0.0 copy-start.1
  137.8 1.0 copy-done.1
Async XLA Ops:
  83.5 52.5 %copy-start = (bf16[256,2048]{1,0:T(8,128)(2,1)S(1)}, bf16[256,2048]{1,0:T(8,128)(2,1)}, u32[]{:S(2)}) copy-start(bf16[256,2048]{1,0:T(8,128)(2,1)} %q_ref.1) | copy-start | bytes 3145732
  83.5 52.5 %copy-start.2 = (s32[256]{0:T(256)S(1)}, s32[256]{0:T(256)}, u32[]{:S(2)}) copy-start(s32[256]{0:T(256)} %param.10) | copy-start | bytes 3076
  83.5 52.5 %copy-start.3 = (s32[256]{0:T(256)S(1)}, s32[256]{0:T(256)}, u32[]{:S(2)}) copy-start(s32[256]{0:T(256)} %param.11) | copy-start | bytes 3076
  104.2 31.8 %all-to-all-start.3 = ((bf16[128,56,128]{2,1,0:T(8,128)(2,1)}), bf16[128,56,128]{2,1,0:T(8,128)(2,1)S(1)}, u32[]{:S(2)}, u32[]{:S(2)}) async-start(bf16[128,56,128]{2,1,0:T(8,128)(2,1)} %get-tuple-element.42), calls=%async_computation.3 | async-start | bytes 3670016 | tf_op jit(solution)/shard_map/all_to_all | solution.py:392
  137.8 1.0 copy-start.1

commit v8 on v7

--- a/solution.py
+++ b/solution.py
@@ -13,13 +13,13 @@
 RUN = 48
 CODES = CL_SET * RUN
 BLK = 128
-FIXED = (4, 5, 6)
+FIXED = (4, 5, 6, 7)
 UNROLL = 16
 TILE = 3
 JOINT = 2
 ALL = 64
 FEW = 56
-PACK = 8
+PACK = 4
 UNPACK = 8
 F32 = jnp.float32
 BF16 = jnp.bfloat16
@@ -46,43 +46,54 @@
     return jnp.dot(a, b, preferred_element_type=F32)
 
 
-def pack_kernel(slots, sets, parity_ref, cid_ref, pos_ref, q_ref, k_ref, v_ref, out_ref, slot_ref, place, meta):
+def pack_kernel(slots, sets, parity_ref, cid_ref, pos_ref, q_hbm, k_hbm, v_hbm, out_ref, slot_ref, x_ref, place, meta, sems):
     tokens = cid_ref.shape[1]
-
-    @pl.when(pl.program_id(0) == 0)
-    def _():
-        cid = cid_ref[...]
-        pos = pos_ref[...]
-        own = jnp.bitwise_and(cid, CL_SET - 1)
-        group = (cid - own).astype(F32) * (1.0 / CL_SET)
-        key = cid.astype(F32) * tokens + iota((1, tokens), 1)
-        keys = column(key)
-        keys = jnp.concatenate([keys] * (tokens // 128), axis=1)
-        below = keys < key
-        rank = jnp.sum(jnp.where(below & (keys >= group * (CL_SET * tokens)), 1.0, 0.0), axis=0, keepdims=True)
-        within = jnp.sum(jnp.where(below & (keys >= cid.astype(F32) * tokens), 1.0, 0.0), axis=0, keepdims=True)
-        fits = rank < slots
-        slot = jnp.where(fits, group * slots + rank, -1.0)
-        slot_ref[...] = slot
-        place[...] = jnp.where(iota((sets * slots, tokens), 0) == slot, 1.0, 0.0).astype(BF16)
-        lane = jnp.where(fits, group * 128 + rank + 64 * parity_ref[0, 0].astype(F32), -1.0)
-        spread = jnp.where(iota((sets * 128, tokens), 0) == lane, 1.0, 0.0).astype(BF16)
-        short = jnp.where(jnp.max(rank, axis=1, keepdims=True) >= slots, 1.0, 0.0)
-        low = jnp.bitwise_and(pos, 255)
-        high = jnp.right_shift(pos, 8) + 1
-        row = lax.broadcasted_iota(jnp.int32, (16, tokens), 0)
-        facts = jnp.where(
-            row == 0,
-            high.astype(F32),
-            jnp.where(row == 1, low.astype(F32), jnp.where(row == 2, own.astype(F32) + 1.0, jnp.where(row == 3, within, 0.0))),
-        ).astype(BF16)
-        meta[...] = nt_dot(facts, spread)
-        meta[4:5, :] = jnp.broadcast_to(short, (1, sets * 128))
+    heads = out_ref.shape[1]
+    steps = heads // PACK
+
+    def part_in(i, j):
+        at = pl.ds(i * PACK * HEAD_DIM, PACK * HEAD_DIM)
+        return pltpu.make_async_copy((q_hbm, k_hbm, v_hbm)[j].at[:, at], x_ref.at[j, :, at], sems.at[i, j])
+
+    for i in range(steps):
+        for j in range(3):
+            part_in(i, j).start()
+
+    cid = cid_ref[...]
+    pos = pos_ref[...]
+    own = jnp.bitwise_and(cid, CL_SET - 1)
+    group = (cid - own).astype(F32) * (1.0 / CL_SET)
+    key = cid.astype(F32) * tokens + iota((1, tokens), 1)
+    keys = column(key)
+    keys = jnp.concatenate([keys] * (tokens // 128), axis=1)
+    below = keys < key
+    rank = jnp.sum(jnp.where(below & (keys >= group * (CL_SET * tokens)), 1.0, 0.0), axis=0, keepdims=True)
+    within = jnp.sum(jnp.where(below & (keys >= cid.astype(F32) * tokens), 1.0, 0.0), axis=0, keepdims=True)
+    fits = rank < slots
+    slot = jnp.where(fits, group * slots + rank, -1.0)
+    slot_ref[...] = slot
+    place[...] = jnp.where(iota((sets * slots, tokens), 0) == slot, 1.0, 0.0).astype(BF16)
+    lane = jnp.where(fits, group * 128 + rank + 64 * parity_ref[0, 0].astype(F32), -1.0)
+    spread = jnp.where(iota((sets * 128, tokens), 0) == lane, 1.0, 0.0).astype(BF16)
+    short = jnp.where(jnp.max(rank, axis=1, keepdims=True) >= slots, 1.0, 0.0)
+    low = jnp.bitwise_and(pos, 255)
+    high = jnp.right_shift(pos, 8) + 1
+    row = lax.broadcasted_iota(jnp.int32, (16, tokens), 0)
+    facts = jnp.where(
+        row == 0,
+        high.astype(F32),
+        jnp.where(row == 1, low.astype(F32), jnp.where(row == 2, own.astype(F32) + 1.0, jnp.where(row == 3, within, 0.0))),
+    ).astype(BF16)
+    meta[...] = nt_dot(facts, spread)
+    meta[4:5, :] = jnp.broadcast_to(short, (1, sets * 128))
 
     gap = out_ref.shape[2] - 3 * slots - 8
-    for h in range(0, out_ref.shape[1], 2):
+    for h in range(0, heads, 2):
+        if h % PACK == 0:
+            for j in range(3):
+                part_in(h // PACK, j).wait()
         at = slice(h * HEAD_DIM, (h + 2) * HEAD_DIM)
-        y = dot(place[...], jnp.concatenate([q_ref[:, at], k_ref[:, at], v_ref[:, at]], axis=1))
+        y = dot(place[...], jnp.concatenate([x_ref[j, :, at] for j in range(3)], axis=1))
         for s in range(sets):
             part = y[s * slots : (s + 1) * slots]
             for u in range(2):
@@ -345,18 +356,22 @@
     tokens, width = queries.shape
     heads = width // HEAD_DIM
     rows = chunk_rows(slots)
-    some = pl.BlockSpec((tokens, PACK * HEAD_DIM), lambda h: (0, h))
-    line = pl.BlockSpec((1, tokens), lambda h: (0, 0))
+    far = pl.BlockSpec(memory_space=pl.ANY)
+    near = pl.BlockSpec(memory_space=pltpu.VMEM)
     return pl.pallas_call(
         functools.partial(pack_kernel, slots, sets),
-        grid=(heads // PACK,),
-        in_specs=[pl.BlockSpec(memory_space=pltpu.SMEM), line, line, some, some, some],
-        out_specs=[pl.BlockSpec((sets, PACK, rows, 128), lambda h: (0, h, 0, 0)), line],
+        in_specs=[pl.BlockSpec(memory_space=pltpu.SMEM), near, near, far, far, far],
+        out_specs=[near, near],
         out_shape=[
-            jax.ShapeDtypeStruct((sets, heads, rows, 128), BF16),
+            pltpu.VMEM((sets, heads, rows, 128), BF16),
             jax.ShapeDtypeStruct((1, tokens), F32),
         ],
-        scratch_shapes=[pltpu.VMEM((sets * slots, tokens), BF16), pltpu.VMEM((16, sets * 128), F32)],
+        scratch_shapes=[
+            pltpu.VMEM((3, tokens, width), BF16),
+            pltpu.VMEM((sets * slots, tokens), BF16),
+            pltpu.VMEM((16, sets * 128), F32),
+            pltpu.SemaphoreType.DMA((heads // PACK, 3)),
+        ],
         compiler_params=pltpu.CompilerParams(vmem_limit_bytes=20 * 2**20),
         name="pack",
     )(parity, cid_row, pos_row, queries, keys, values)
@@ -373,7 +388,7 @@
             pl.BlockSpec((sets, UNPACK, slots, 128), lambda h: (0, h, 0, 0)),
         ],
         out_specs=pl.BlockSpec((tokens, UNPACK * HEAD_DIM), lambda h: (0, h)),
-        out_shape=jax.ShapeDtypeStruct((tokens, heads * HEAD_DIM), BF16),
+        out_shape=pltpu.HBM((tokens, heads * HEAD_DIM), BF16),
         scratch_shapes=[pltpu.VMEM((tokens, sets * slots), BF16)],
         compiler_params=pltpu.CompilerParams(vmem_limit_bytes=16 * 2**20),
         name="unpack",

time: 140 us -> 150 us (1.071); the launches traced: 139 us -> 152 us
  starting transfers between devices: 5.04 us -> 20.7 us
  Pallas kernels: 26.4 us -> 24.8 us
    all_to_all x1, starting transfers between devices: 5.04 us -> 20.7 us  [attention(): lax.all_to_all(done, ('grp', 'blk'), split_axis=0, concat_axis=0, tiled=T...]
    pallas_call x1, Pallas kernels: 20.7 us -> 18.1 us  [attend_call(): pl.pallas_call(functools.partial(attend_kernel, slots), in_specs=[whole],...]
where the time goes in v8:
time: 150 us; the launch traced here: 152 us
  blocking collectives  79.5 us (53%)
  waiting for transfers between devices  25.4 us (17%)
  Pallas kernels  24.8 us (17%)
  starting transfers between devices  20.7 us (14%)
    all_to_all x1, blocking collectives, attention(): lax.all_to_all(sent.reshape(sources, sent.shape[2], 128), ('grp', 'blk'),...  79.5 us
    all_to_all x1, waiting for transfers between devices, attention(): lax.all_to_all(done, ('grp', 'blk'), split_axis=0, concat_axis=0, tiled=T...  25.4 us
    all_to_all x1, starting transfers between devices, attention(): lax.all_to_all(done, ('grp', 'blk'), split_axis=0, concat_axis=0, tiled=T...  20.7 us
    pallas_call x1, Pallas kernels, attend_call(): pl.pallas_call(functools.partial(attend_kernel, slots), in_specs=[whole],...  18.1 us
    pallas_call x1, Pallas kernels, pack_call(): pl.pallas_call(functools.partial(pack_kernel, slots, sets), in_specs=[pl....  4.21 us
  transfers between devices with their start and end apart: 1, of which 1 were waited for; matrix products, arithmetic and copies ran while one was open for 0% of the time, Pallas kernels for 0%

profile of v8, /device:TPU:0, one launch (start us, length us, event | category | flops | bytes accessed | tf_op | source)
XLA Modules:
  0.0 151.8 jit_solution(18218309490856899397)
XLA Ops:
  0.0 4.2 %pack.3 = (bf16[8,16,176,128]{3,2,1,0:T(8,128)(2,1)S(1)}, f32[1,256]{1,0:T(1,128)S(1)}) custom-call(s32[1,1]{1,0:T(1,128)} %bitcast.3.parity_ref, s32[1,256]{1,0:T(1,128)} %bitcast.12, s32[1,256]{1,0:T(1,128)} %bitcast.14, bf16[256,2048]{1,0:T(8,128)(2,1)} %q_hbm.1, bf16[256,2048]{1,0:T(8,128)(2,1)} %k_hbm.1, bf16[256,2048]{1,0:T(8,128)(2,1)} %v_hbm.1), custom_call_target="tpu_custom_call" | custom-call | tf_op jit(solution)/shard_map/pack/pallas_call | solution.py:361
  4.2 79.5 %all_to_all.20.x_ref = bf16[128,176,128]{2,1,0:T(8,128)(2,1)S(1)} all-to-all(bf16[128,176,128]{2,1,0:T(8,128)(2,1)S(1)} %bitcast.10), channel_id=1, replica_groups=mesh['grp'=16,'blk'=8] {'grp','blk'}, dimensions={0} | all-to-all | bytes 11534336 | tf_op jit(solution)/shard_map/all_to_all | solution.py:403
  83.8 0.0 copy-start
  83.8 0.0 copy-start.1
  83.8 0.0 copy-start.2
  83.8 18.1 %attend.3 = (bf16[128,56,128]{2,1,0:T(8,128)(2,1)}, f32[8,128]{1,0:T(8,128)S(1)}) custom-call(bf16[128,176,128]{2,1,0:T(8,128)(2,1)S(1)} %all_to_all.20.x_ref), custom_call_target="tpu_custom_call" | custom-call | tf_op jit(solution)/shard_map/attend/pallas_call | solution.py:317
  101.9 20.7 %all-to-all-start.3 = ((bf16[128,56,128]{2,1,0:T(8,128)(2,1)}), bf16[128,56,128]{2,1,0:T(8,128)(2,1)S(1)}, u32[]{:S(2)}, u32[]{:S(2)}) async-start(bf16[128,56,128]{2,1,0:T(8,128)(2,1)} %get-tuple-element.42), calls=%async_computation.3 | async-start | bytes 3670016 | tf_op jit(solution)/shard_map/all_to_all | solution.py:407
  122.6 0.5 slice.3
  123.8 25.4 %all-to-all-done.3 = bf16[128,56,128]{2,1,0:T(8,128)(2,1)S(1)} async-done(((bf16[128,56,128]{2,1,0:T(8,128)(2,1)}), bf16[128,56,128]{2,1,0:T(8,128)(2,1)S(1)}, u32[]{:S(2)}, u32[]{:S(2)}) %all-to-all-start.3) | async-done | bytes 1835040 | tf_op jit(solution)/shard_map/all_to_all | solution.py:407
  149.1 0.0 copy-done
  149.1 0.0 copy-done.1
  149.1 0.0 copy-done.2
  149.2 2.5 %conditional.1 = (bf16[256,2048]{1,0:T(8,128)(2,1)}) conditional(s32[]{:T(128)} %bitcast.7, (bf16[128,56,128]{2,1,0:T(8,128)(2,1)S(1)}, f32[1,256]{1,0:T(1,128)S(1)}) %tuple.11, (s32[1,1]{1,0:T(1,128)}, s32[1,256]{1,0:T(1,128)S(1)}, s32[1,256]{1,0:T(1,128)S(1)}, bf16[256,2048]{1,0:T(8,128)(2,1)S(1)}, bf16[256,2048]{1,0:T(8,128)(2,1)}, ...), branch_computations={%region_0.1_spmd, %region_1.2_spmd} | conditional | bytes 17825800 | solution.py:411
  149.2 2.5 %unpack.2 = bf16[256,2048]{1,0:T(8,128)(2,1)} custom-call(f32[1,256]{1,0:T(1,128)S(1)} %get-tuple-element.25.slot_ref, bf16[8,16,56,128]{3,2,1,0:T(8,128)(2,1)S(1)} %bitcast.11), custom_call_target="tpu_custom_call" | custom-call | tf_op jit(solution)/shard_map/cond/branch_0_fun/unpack/pallas_call | solution.py:383
Async XLA Ops:
  83.8 65.4 %copy-start = (bf16[256,2048]{1,0:T(8,128)(2,1)S(1)}, bf16[256,2048]{1,0:T(8,128)(2,1)}, u32[]{:S(2)}) copy-start(bf16[256,2048]{1,0:T(8,128)(2,1)} %q_hbm.1) | copy-start | bytes 3145732
  83.8 65.4 %copy-start.1 = (s32[256]{0:T(256)S(1)}, s32[256]{0:T(256)}, u32[]{:S(2)}) copy-start(s32[256]{0:T(256)} %param.10) | copy-start | bytes 3076
  83.8 65.4 %copy-start.2 = (s32[256]{0:T(256)S(1)}, s32[256]{0:T(256)}, u32[]{:S(2)}) copy-start(s32[256]{0:T(256)} %param.11) | copy-start | bytes 3076
  101.9 47.3 %all-to-all-start.3 = ((bf16[128,56,128]{2,1,0:T(8,128)(2,1)}), bf16[128,56,128]{2,1,0:T(8,128)(2,1)S(1)}, u32[]{:S(2)}, u32[]{:S(2)}) async-start(bf16[128,56,128]{2,1,0:T(8,128)(2,1)} %get-tuple-element.42), calls=%async_computation.3 | async-start | bytes 3670016 | tf_op jit(solution)/shard_map/all_to_all | solution.py:407

commit v9 on v7

--- a/solution.py
+++ b/solution.py
@@ -13,7 +13,7 @@
 RUN = 48
 CODES = CL_SET * RUN
 BLK = 128
-FIXED = (4, 5, 6)
+FIXED = (4, 5, 6, 7)
 UNROLL = 16
 TILE = 3
 JOINT = 2

time: 140 us -> 151 us (1.079); the launches traced: 139 us -> 154 us
  starting transfers between devices: 5.04 us -> 22.4 us
  Pallas kernels: 26.4 us -> 23.8 us
    all_to_all x1, starting transfers between devices: 5.04 us -> 22.4 us  [attention(): lax.all_to_all(done, ('grp', 'blk'), split_axis=0, concat_axis=0, tiled=T...]
    pallas_call x1, Pallas kernels: 20.7 us -> 18.1 us  [attend_call(): pl.pallas_call(functools.partial(attend_kernel, slots), in_specs=[whole],...]
where the time goes in v9:
time: 151 us; the launch traced here: 154 us
  blocking collectives  79.5 us (53%)
  waiting for transfers between devices  25.4 us (17%)
  Pallas kernels  23.8 us (16%)
  starting transfers between devices  22.4 us (15%)
    all_to_all x1, blocking collectives, attention(): lax.all_to_all(sent.reshape(sources, sent.shape[2], 128), ('grp', 'blk'),...  79.5 us
    all_to_all x1, waiting for transfers between devices, attention(): lax.all_to_all(done, ('grp', 'blk'), split_axis=0, concat_axis=0, tiled=T...  25.4 us
    all_to_all x1, starting transfers between devices, attention(): lax.all_to_all(done, ('grp', 'blk'), split_axis=0, concat_axis=0, tiled=T...  22.4 us
    pallas_call x1, Pallas kernels, attend_call(): pl.pallas_call(functools.partial(attend_kernel, slots), in_specs=[whole],...  18.1 us
    pallas_call x1, Pallas kernels, pack_call(): pl.pallas_call(functools.partial(pack_kernel, slots, sets), grid=(heads /...  3.97 us
  transfers between devices with their start and end apart: 1, of which 1 were waited for; matrix products, arithmetic and copies ran while one was open for 0% of the time, Pallas kernels for 0%

profile of v9, /device:TPU:0, one launch (start us, length us, event | category | flops | bytes accessed | tf_op | source)
XLA Modules:
  0.0 153.5 jit_solution(18150406901783721555)
XLA Ops:
  0.0 4.0 %pack.3 = (bf16[8,16,176,128]{3,2,1,0:T(8,128)(2,1)S(1)}, f32[1,256]{1,0:T(1,128)S(1)}) custom-call(s32[1,1]{1,0:T(1,128)} %bitcast.3.parity_ref, s32[1,256]{1,0:T(1,128)} %bitcast.12, s32[1,256]{1,0:T(1,128)} %bitcast.14, bf16[256,2048]{1,0:T(8,128)(2,1)} %q_ref.1, bf16[256,2048]{1,0:T(8,128)(2,1)} %k_ref.1, bf16[256,2048]{1,0:T(8,128)(2,1)} %v_ref.1), custom_call_target="tpu_custom_call" | custom-call | tf_op jit(solution)/shard_map/pack/pallas_call | solution.py:350
  4.0 79.5 %all_to_all.20.x_ref = bf16[128,176,128]{2,1,0:T(8,128)(2,1)S(1)} all-to-all(bf16[128,176,128]{2,1,0:T(8,128)(2,1)S(1)} %bitcast.10), channel_id=1, replica_groups=mesh['grp'=16,'blk'=8] {'grp','blk'}, dimensions={0} | all-to-all | bytes 11534336 | tf_op jit(solution)/shard_map/all_to_all | solution.py:388
  83.5 0.0 copy-start
  83.5 0.0 copy-start.2
  83.5 0.0 copy-start.3
  83.5 18.1 %attend.3 = (bf16[128,56,128]{2,1,0:T(8,128)(2,1)}, f32[8,128]{1,0:T(8,128)S(1)}) custom-call(bf16[128,176,128]{2,1,0:T(8,128)(2,1)S(1)} %all_to_all.20.x_ref), custom_call_target="tpu_custom_call" | custom-call | tf_op jit(solution)/shard_map/attend/pallas_call | solution.py:306
  101.6 22.4 %all-to-all-start.3 = ((bf16[128,56,128]{2,1,0:T(8,128)(2,1)}), bf16[128,56,128]{2,1,0:T(8,128)(2,1)S(1)}, u32[]{:S(2)}, u32[]{:S(2)}) async-start(bf16[128,56,128]{2,1,0:T(8,128)(2,1)} %get-tuple-element.42), calls=%async_computation.3 | async-start | bytes 3670016 | tf_op jit(solution)/shard_map/all_to_all | solution.py:392
  124.1 0.5 slice.3
  125.3 25.4 %all-to-all-done.3 = bf16[128,56,128]{2,1,0:T(8,128)(2,1)S(1)} async-done(((bf16[128,56,128]{2,1,0:T(8,128)(2,1)}), bf16[128,56,128]{2,1,0:T(8,128)(2,1)S(1)}, u32[]{:S(2)}, u32[]{:S(2)}) %all-to-all-start.3) | async-done | bytes 1835040 | tf_op jit(solution)/shard_map/all_to_all | solution.py:392
  150.6 0.0 copy-done
  150.6 0.0 copy-done.2
  150.6 0.0 copy-done.3
  150.6 1.8 %conditional.1 = (bf16[256,2048]{1,0:T(8,128)(2,1)S(1)}) conditional(s32[]{:T(128)} %bitcast.7, (bf16[128,56,128]{2,1,0:T(8,128)(2,1)S(1)}, f32[1,256]{1,0:T(1,128)S(1)}) %tuple.11, (s32[1,1]{1,0:T(1,128)}, s32[1,256]{1,0:T(1,128)S(1)}, s32[1,256]{1,0:T(1,128)S(1)}, bf16[256,2048]{1,0:T(8,128)(2,1)S(1)}, bf16[256,2048]{1,0:T(8,128)(2,1)}, ...), branch_computations={%region_0.1_spmd, %region_1.2_spmd} | conditional | bytes 17825800 | solution.py:396
  150.6 1.7 %unpack.2 = bf16[256,2048]{1,0:T(8,128)(2,1)S(1)} custom-call(f32[1,256]{1,0:T(1,128)S(1)} %get-tuple-element.25.slot_ref, bf16[8,16,56,128]{3,2,1,0:T(8,128)(2,1)S(1)} %bitcast.11), custom_call_target="tpu_custom_call" | custom-call | tf_op jit(solution)/shard_map/cond/branch_0_fun/unpack/pallas_call | solution.py:368
  152.4 0.0 copy-start.1
  152.4 1.0 copy-done.1
Async XLA Ops:
  83.5 67.1 %copy-start = (bf16[256,2048]{1,0:T(8,128)(2,1)S(1)}, bf16[256,2048]{1,0:T(8,128)(2,1)}, u32[]{:S(2)}) copy-start(bf16[256,2048]{1,0:T(8,128)(2,1)} %q_ref.1) | copy-start | bytes 3145732
  83.5 67.1 %copy-start.2 = (s32[256]{0:T(256)S(1)}, s32[256]{0:T(256)}, u32[]{:S(2)}) copy-start(s32[256]{0:T(256)} %param.10) | copy-start | bytes 3076
  83.5 67.1 %copy-start.3 = (s32[256]{0:T(256)S(1)}, s32[256]{0:T(256)}, u32[]{:S(2)}) copy-start(s32[256]{0:T(256)} %param.11) | copy-start | bytes 3076
  101.6 49.0 %all-to-all-start.3 = ((bf16[128,56,128]{2,1,0:T(8,128)(2,1)}), bf16[128,56,128]{2,1,0:T(8,128)(2,1)S(1)}, u32[]{:S(2)}, u32[]{:S(2)}) async-start(bf16[128,56,128]{2,1,0:T(8,128)(2,1)} %get-tuple-element.42), calls=%async_computation.3 | async-start | bytes 3670016 | tf_op jit(solution)/shard_map/all_to_all | solution.py:392
  152.4 1.0 copy-start.1

commit v10 on v9

--- a/solution.py
+++ b/solution.py
@@ -14,6 +14,7 @@
 CODES = CL_SET * RUN
 BLK = 128
 FIXED = (4, 5, 6, 7)
+FIXED_SHORT = (6,)
 UNROLL = 16
 TILE = 3
 JOINT = 2
@@ -97,6 +98,7 @@
     sources, rows, _ = x_ref.shape
     blocks = sources // 4
     total_rows = xs.shape[0]
+    whole_counts, unroll = (FIXED, UNROLL) if slots == FEW else (FIXED_SHORT, 2)
     os[...] = jnp.zeros(os.shape, BF16)
     ahead = 5 * sources // 16
     xs[0 : ahead * BLK, :] = jnp.zeros((ahead * BLK, xs.shape[1]), BF16)
@@ -188,13 +190,13 @@
 
     def each_block(body):
         def some(i, _):
-            for u in range(UNROLL):
-                body(i * UNROLL + u, 0)
+            for u in range(unroll):
+                body(i * unroll + u, 0)
 
             @pl.when(most_passes > 1)
             def _():
                 def rest(u, _):
-                    b = i * UNROLL + u
+                    b = i * unroll + u
 
                     def more(p, _):
                         body(b, p)
@@ -202,11 +204,11 @@
 
                     return lax.fori_loop(1, passes_of(b), more, 0)
 
-                lax.fori_loop(0, UNROLL, rest, 0)
+                lax.fori_loop(0, unroll, rest, 0)
 
             return 0
 
-        lax.fori_loop(0, blocks // UNROLL, some, 0)
+        lax.fori_loop(0, blocks // unroll, some, 0)
 
     each_block(compact)
 
@@ -267,11 +269,15 @@
         counts = [count_of(c) for c in pair]
         most = functools.reduce(jnp.maximum, counts)
         least = functools.reduce(jnp.minimum, counts)
-        alike = (most >= FIXED[0]) & (most <= FIXED[-1]) & (least >= most - 2)
-        for n in FIXED:
-            pl.when(alike & (most == n))(functools.partial(fixed, pair, n))
-
-        @pl.when(jnp.logical_not(alike))
+        done = jnp.bool_(False)
+        smaller = whole_counts[0] - 2
+        for n in whole_counts:
+            alike = (most > smaller) & (most <= n) & (least >= n - 2)
+            pl.when(alike)(functools.partial(fixed, pair, n))
+            done = done | alike
+            smaller = n
+
+        @pl.when(jnp.logical_not(done))
         def _():
             for c, n in zip(pair, counts):
                 general(begin_of(c), n)

time: 151 us -> 139 us (0.921); the launches traced: 154 us -> 138 us
  starting transfers between devices: 22.4 us -> 7.15 us
    all_to_all x1, starting transfers between devices: 22.4 us -> 7.15 us  [attention(): lax.all_to_all(done, ('grp', 'blk'), split_axis=0, concat_axis=0, tiled=T...]
where the time goes in v10:
time: 139 us; the launch traced here: 138 us
  blocking collectives  79.5 us (57%)
  waiting for transfers between devices  25.4 us (18%)
  Pallas kernels  23.7 us (17%)
  starting transfers between devices  7.15 us (5%)
  local copies, waits for them, and re-layouts  1.49 us (1%)
    all_to_all x1, blocking collectives, attention(): lax.all_to_all(sent.reshape(sources, sent.shape[2], 128), ('grp', 'blk'),...  79.5 us
    all_to_all x1, waiting for transfers between devices, attention(): lax.all_to_all(done, ('grp', 'blk'), split_axis=0, concat_axis=0, tiled=T...  25.4 us
    pallas_call x1, Pallas kernels, attend_call(): pl.pallas_call(functools.partial(attend_kernel, slots), in_specs=[whole],...  18 us
    all_to_all x1, starting transfers between devices, attention(): lax.all_to_all(done, ('grp', 'blk'), split_axis=0, concat_axis=0, tiled=T...  7.15 us
    pallas_call x1, Pallas kernels, pack_call(): pl.pallas_call(functools.partial(pack_kernel, slots, sets), grid=(heads /...  3.96 us
  transfers between devices with their start and end apart: 1, of which 1 were waited for; matrix products, arithmetic and copies ran while one was open for 0% of the time, Pallas kernels for 0%

profile of v10, /device:TPU:0, one launch (start us, length us, event | category | flops | bytes accessed | tf_op | source)
XLA Modules:
  0.0 138.0 jit_solution(2559572410291144705)
XLA Ops:
  0.0 4.0 %pack.3 = (bf16[8,16,176,128]{3,2,1,0:T(8,128)(2,1)S(1)}, f32[1,256]{1,0:T(1,128)S(1)}) custom-call(s32[1,1]{1,0:T(1,128)} %bitcast.3.parity_ref, s32[1,256]{1,0:T(1,128)} %bitcast.12, s32[1,256]{1,0:T(1,128)} %bitcast.14, bf16[256,2048]{1,0:T(8,128)(2,1)} %q_ref.1, bf16[256,2048]{1,0:T(8,128)(2,1)} %k_ref.1, bf16[256,2048]{1,0:T(8,128)(2,1)} %v_ref.1), custom_call_target="tpu_custom_call" | custom-call | tf_op jit(solution)/shard_map/pack/pallas_call | solution.py:356
  4.0 79.5 %all_to_all.20.x_ref = bf16[128,176,128]{2,1,0:T(8,128)(2,1)S(1)} all-to-all(bf16[128,176,128]{2,1,0:T(8,128)(2,1)S(1)} %bitcast.10), channel_id=1, replica_groups=mesh['grp'=16,'blk'=8] {'grp','blk'}, dimensions={0} | all-to-all | bytes 11534336 | tf_op jit(solution)/shard_map/all_to_all | solution.py:394
  83.5 0.0 copy-start
  83.5 0.0 copy-start.2
  83.5 0.0 copy-start.3
  83.5 18.0 %attend.3 = (bf16[128,56,128]{2,1,0:T(8,128)(2,1)}, f32[8,128]{1,0:T(8,128)S(1)}) custom-call(bf16[128,176,128]{2,1,0:T(8,128)(2,1)S(1)} %all_to_all.20.x_ref), custom_call_target="tpu_custom_call" | custom-call | tf_op jit(solution)/shard_map/attend/pallas_call | solution.py:312
  101.6 7.2 %all-to-all-start.3 = ((bf16[128,56,128]{2,1,0:T(8,128)(2,1)}), bf16[128,56,128]{2,1,0:T(8,128)(2,1)S(1)}, u32[]{:S(2)}, u32[]{:S(2)}) async-start(bf16[128,56,128]{2,1,0:T(8,128)(2,1)} %get-tuple-element.42), calls=%async_computation.3 | async-start | bytes 3670016 | tf_op jit(solution)/shard_map/all_to_all | solution.py:398
  108.7 0.5 slice.3
  109.9 25.4 %all-to-all-done.3 = bf16[128,56,128]{2,1,0:T(8,128)(2,1)S(1)} async-done(((bf16[128,56,128]{2,1,0:T(8,128)(2,1)}), bf16[128,56,128]{2,1,0:T(8,128)(2,1)S(1)}, u32[]{:S(2)}, u32[]{:S(2)}) %all-to-all-start.3) | async-done | bytes 1835040 | tf_op jit(solution)/shard_map/all_to_all | solution.py:398
  135.3 0.0 copy-done
  135.3 0.0 copy-done.2
  135.3 0.0 copy-done.3
  135.3 1.8 %conditional.1 = (bf16[256,2048]{1,0:T(8,128)(2,1)S(1)}) conditional(s32[]{:T(128)} %bitcast.7, (bf16[128,56,128]{2,1,0:T(8,128)(2,1)S(1)}, f32[1,256]{1,0:T(1,128)S(1)}) %tuple.11, (s32[1,1]{1,0:T(1,128)}, s32[1,256]{1,0:T(1,128)S(1)}, s32[1,256]{1,0:T(1,128)S(1)}, bf16[256,2048]{1,0:T(8,128)(2,1)S(1)}, bf16[256,2048]{1,0:T(8,128)(2,1)}, ...), branch_computations={%region_0.1_spmd, %region_1.2_spmd} | conditional | bytes 17825800 | solution.py:402
  135.3 1.7 %unpack.2 = bf16[256,2048]{1,0:T(8,128)(2,1)S(1)} custom-call(f32[1,256]{1,0:T(1,128)S(1)} %get-tuple-element.25.slot_ref, bf16[8,16,56,128]{3,2,1,0:T(8,128)(2,1)S(1)} %bitcast.11), custom_call_target="tpu_custom_call" | custom-call | tf_op jit(solution)/shard_map/cond/branch_0_fun/unpack/pallas_call | solution.py:374
  137.1 0.0 copy-start.1
  137.1 1.0 copy-done.1
Async XLA Ops:
  83.5 51.8 %copy-start = (bf16[256,2048]{1,0:T(8,128)(2,1)S(1)}, bf16[256,2048]{1,0:T(8,128)(2,1)}, u32[]{:S(2)}) copy-start(bf16[256,2048]{1,0:T(8,128)(2,1)} %q_ref.1) | copy-start | bytes 3145732
  83.5 51.8 %copy-start.2 = (s32[256]{0:T(256)S(1)}, s32[256]{0:T(256)}, u32[]{:S(2)}) copy-start(s32[256]{0:T(256)} %param.10) | copy-start | bytes 3076
  83.5 51.8 %copy-start.3 = (s32[256]{0:T(256)S(1)}, s32[256]{0:T(256)}, u32[]{:S(2)}) copy-start(s32[256]{0:T(256)} %param.11) | copy-start | bytes 3076
  101.6 33.7 %all-to-all-start.3 = ((bf16[128,56,128]{2,1,0:T(8,128)(2,1)}), bf16[128,56,128]{2,1,0:T(8,128)(2,1)S(1)}, u32[]{:S(2)}, u32[]{:S(2)}) async-start(bf16[128,56,128]{2,1,0:T(8,128)(2,1)} %get-tuple-element.42), calls=%async_computation.3 | async-start | bytes 3670016 | tf_op jit(solution)/shard_map/all_to_all | solution.py:398
  137.1 1.0 copy-start.1

commit v11 on v10

--- a/solution.py
+++ b/solution.py
@@ -15,7 +15,7 @@
 BLK = 128
 FIXED = (4, 5, 6, 7)
 FIXED_SHORT = (6,)
-UNROLL = 16
+UNROLL = 32
 TILE = 3
 JOINT = 2
 ALL = 64
@@ -379,7 +379,7 @@
             pl.BlockSpec((sets, UNPACK, slots, 128), lambda h: (0, h, 0, 0)),
         ],
         out_specs=pl.BlockSpec((tokens, UNPACK * HEAD_DIM), lambda h: (0, h)),
-        out_shape=jax.ShapeDtypeStruct((tokens, heads * HEAD_DIM), BF16),
+        out_shape=pltpu.HBM((tokens, heads * HEAD_DIM), BF16),
         scratch_shapes=[pltpu.VMEM((tokens, sets * slots), BF16)],
         compiler_params=pltpu.CompilerParams(vmem_limit_bytes=16 * 2**20),
         name="unpack",

time: 139 us -> 138 us (level); the launches traced: 138 us -> 139 us
  Pallas kernels: 23.7 us -> 27.6 us
  starting transfers between devices: 7.15 us -> 5.06 us
    pallas_call x1, Pallas kernels: 18 us -> 21.2 us  [attend_call(): pl.pallas_call(functools.partial(attend_kernel, slots), in_specs=[whole],...]
    all_to_all x1, starting transfers between devices: 7.15 us -> 5.06 us  [attention(): lax.all_to_all(done, ('grp', 'blk'), split_axis=0, concat_axis=0, tiled=T...]
where the time goes in v11:
time: 138 us; the launch traced here: 139 us
  blocking collectives  79.5 us (58%)
  Pallas kernels  27.6 us (20%)
  waiting for transfers between devices  25.6 us (19%)
  starting transfers between devices  5.06 us (4%)
    all_to_all x1, blocking collectives, attention(): lax.all_to_all(sent.reshape(sources, sent.shape[2], 128), ('grp', 'blk'),...  79.5 us
    all_to_all x1, waiting for transfers between devices, attention(): lax.all_to_all(done, ('grp', 'blk'), split_axis=0, concat_axis=0, tiled=T...  25.6 us
    pallas_call x1, Pallas kernels, attend_call(): pl.pallas_call(functools.partial(attend_kernel, slots), in_specs=[whole],...  21.2 us
    all_to_all x1, starting transfers between devices, attention(): lax.all_to_all(done, ('grp', 'blk'), split_axis=0, concat_axis=0, tiled=T...  5.06 us
    pallas_call x1, Pallas kernels, pack_call(): pl.pallas_call(functools.partial(pack_kernel, slots, sets), grid=(heads /...  3.96 us
  transfers between devices with their start and end apart: 1, of which 1 were waited for; matrix products, arithmetic and copies ran while one was open for 0% of the time, Pallas kernels for 0%

profile of v11, /device:TPU:0, one launch (start us, length us, event | category | flops | bytes accessed | tf_op | source)
XLA Modules:
  0.0 139.1 jit_solution(11616678721630841101)
XLA Ops:
  0.0 4.0 %pack.3 = (bf16[8,16,176,128]{3,2,1,0:T(8,128)(2,1)S(1)}, f32[1,256]{1,0:T(1,128)S(1)}) custom-call(s32[1,1]{1,0:T(1,128)} %bitcast.3.parity_ref, s32[1,256]{1,0:T(1,128)} %bitcast.12, s32[1,256]{1,0:T(1,128)} %bitcast.14, bf16[256,2048]{1,0:T(8,128)(2,1)} %q_ref.1, bf16[256,2048]{1,0:T(8,128)(2,1)} %k_ref.1, bf16[256,2048]{1,0:T(8,128)(2,1)} %v_ref.1), custom_call_target="tpu_custom_call" | custom-call | tf_op jit(solution)/shard_map/pack/pallas_call | solution.py:356
  4.0 79.5 %all_to_all.20.x_ref = bf16[128,176,128]{2,1,0:T(8,128)(2,1)S(1)} all-to-all(bf16[128,176,128]{2,1,0:T(8,128)(2,1)S(1)} %bitcast.10), channel_id=1, replica_groups=mesh['grp'=16,'blk'=8] {'grp','blk'}, dimensions={0} | all-to-all | bytes 11534336 | tf_op jit(solution)/shard_map/all_to_all | solution.py:394
  83.5 0.0 copy-start
  83.5 0.0 copy-start.1
  83.5 0.0 copy-start.2
  83.5 21.2 %attend.3 = (bf16[128,56,128]{2,1,0:T(8,128)(2,1)}, f32[8,128]{1,0:T(8,128)S(1)}) custom-call(bf16[128,176,128]{2,1,0:T(8,128)(2,1)S(1)} %all_to_all.20.x_ref), custom_call_target="tpu_custom_call" | custom-call | tf_op jit(solution)/shard_map/attend/pallas_call | solution.py:312
  104.7 5.1 %all-to-all-start.3 = ((bf16[128,56,128]{2,1,0:T(8,128)(2,1)}), bf16[128,56,128]{2,1,0:T(8,128)(2,1)S(1)}, u32[]{:S(2)}, u32[]{:S(2)}) async-start(bf16[128,56,128]{2,1,0:T(8,128)(2,1)} %get-tuple-element.42), calls=%async_computation.3 | async-start | bytes 3670016 | tf_op jit(solution)/shard_map/all_to_all | solution.py:398
  109.8 0.5 slice.3
  111.0 25.6 %all-to-all-done.3 = bf16[128,56,128]{2,1,0:T(8,128)(2,1)S(1)} async-done(((bf16[128,56,128]{2,1,0:T(8,128)(2,1)}), bf16[128,56,128]{2,1,0:T(8,128)(2,1)S(1)}, u32[]{:S(2)}, u32[]{:S(2)}) %all-to-all-start.3) | async-done | bytes 1835040 | tf_op jit(solution)/shard_map/all_to_all | solution.py:398
  136.6 0.0 copy-done
  136.6 0.0 copy-done.1
  136.6 0.0 copy-done.2
  136.6 2.5 %conditional.1 = (bf16[256,2048]{1,0:T(8,128)(2,1)}) conditional(s32[]{:T(128)} %bitcast.7, (bf16[128,56,128]{2,1,0:T(8,128)(2,1)S(1)}, f32[1,256]{1,0:T(1,128)S(1)}) %tuple.11, (s32[1,1]{1,0:T(1,128)}, s32[1,256]{1,0:T(1,128)S(1)}, s32[1,256]{1,0:T(1,128)S(1)}, bf16[256,2048]{1,0:T(8,128)(2,1)S(1)}, bf16[256,2048]{1,0:T(8,128)(2,1)}, ...), branch_computations={%region_0.1_spmd, %region_1.2_spmd} | conditional | bytes 17825800 | solution.py:402
  136.6 2.5 %unpack.2 = bf16[256,2048]{1,0:T(8,128)(2,1)} custom-call(f32[1,256]{1,0:T(1,128)S(1)} %get-tuple-element.25.slot_ref, bf16[8,16,56,128]{3,2,1,0:T(8,128)(2,1)S(1)} %bitcast.11), custom_call_target="tpu_custom_call" | custom-call | tf_op jit(solution)/shard_map/cond/branch_0_fun/unpack/pallas_call | solution.py:374
Async XLA Ops:
  83.5 53.0 %copy-start = (bf16[256,2048]{1,0:T(8,128)(2,1)S(1)}, bf16[256,2048]{1,0:T(8,128)(2,1)}, u32[]{:S(2)}) copy-start(bf16[256,2048]{1,0:T(8,128)(2,1)} %q_ref.1) | copy-start | bytes 3145732
  83.5 53.1 %copy-start.1 = (s32[256]{0:T(256)S(1)}, s32[256]{0:T(256)}, u32[]{:S(2)}) copy-start(s32[256]{0:T(256)} %param.10) | copy-start | bytes 3076
  83.5 53.1 %copy-start.2 = (s32[256]{0:T(256)S(1)}, s32[256]{0:T(256)}, u32[]{:S(2)}) copy-start(s32[256]{0:T(256)} %param.11) | copy-start | bytes 3076
  104.7 31.8 %all-to-all-start.3 = ((bf16[128,56,128]{2,1,0:T(8,128)(2,1)}), bf16[128,56,128]{2,1,0:T(8,128)(2,1)S(1)}, u32[]{:S(2)}, u32[]{:S(2)}) async-start(bf16[128,56,128]{2,1,0:T(8,128)(2,1)} %get-tuple-element.42), calls=%async_computation.3 | async-start | bytes 3670016 | tf_op jit(solution)/shard_map/all_to_all | solution.py:398
